TPU v7x, 256 devices: a whole 4x4x8 slice. The times are simulated.
256 devices in a mesh: tile: 64 (over x, z, y_hi), kern: 4 (over y_lo, core).
Axes of the slice: x: 4, y: 4 (y_hi: 2, y_lo: 2; y = y_hi * 2 + y_lo), z: 8, core: 2. Of those that a mesh axis runs over, the one named last changes fastest.
Arguments:
- mask: float32 [4096, 2048], P('tile'), may hold values from -1 to 1
- target: float32 [4096, 2048], P('tile'), may hold values from 0 to 1
- spectra: float32 [24, 16, 128], P('kern'), may hold values from -64 to 64
- weights: float32 [24], P('kern'), may hold values from 0.1 to 1
- counts: int32 [64], P('tile'), may hold values from 32 to 256, as said below
- frag_rows: int32 [16384], P('tile'), may hold values from 0 to 63
- frag_cols: int32 [16384], P('tile'), may hold values from 0 to 2016
- step: float32 [16384], P('tile'), may hold values from -6 to 6
Outputs:
- gradient: float32 [16384], P('tile')
- curvature: float32 [16384], P('tile')
Inputs may be any that keep to these rules, and one draw needn't show every extreme that they name: `counts`: the used slots of a slab are its first ones; in every draw some slab uses all 256.
All inputs are finite; a program needn't handle non-finite values.
Results may differ from a plain program's by a relative error of at most 0.0003.
Values sent between devices are 32-bit elements; how exact they have to be, the bound alone decides.
A program may use at most 128 MiB of HBM per device.

v0:
```python
import functools
import math

import jax
import jax.numpy as jnp
import ml_dtypes
import numpy as np
from jax import lax
from jax.experimental import pallas as pl
from jax.experimental.pallas import tpu as pltpu
from jax.sharding import PartitionSpec as P

WIDTH = 2048
COL_FREQS = 64
ROW_FREQS = 16
KERNELS = 24
FRAG_LEN = 32
SLAB = 64
SLOTS = 256
EXT = 192
TILES = 64
KERN = 4
LOCAL = KERNELS // KERN
GRID_ROWS = 32
GRID_COLS = 128
STEEP = 10.0
THRESH = 0.1
F32 = jnp.float32
BF16 = jnp.bfloat16
CHUNKS = 4
MESH = pl.DeviceIdType.MESH


def np_split(x):
    hi = x.astype(np.float32).astype(ml_dtypes.bfloat16)
    lo = (x - hi.astype(np.float64)).astype(np.float32).astype(ml_dtypes.bfloat16)
    return hi, lo


def pad_lanes(x, lanes=256):
    return np.pad(x, ((0, 0), (0, lanes - x.shape[1])))


@functools.lru_cache(maxsize=None)
def make_tables():
    kc = np.arange(COL_FREQS) - COL_FREQS // 2
    kr = np.arange(ROW_FREQS) - ROW_FREQS // 2
    x = np.arange(WIDTH)
    ang = 2 * np.pi * (np.outer(x, kc) % WIDTH) / WIDTH
    f_hi, f_lo = np_split(np.concatenate([np.cos(ang), -np.sin(ang)], 1) / math.sqrt(WIDTH))
    fwd = np.concatenate([f_hi, f_lo], 1)

    n = np.arange(GRID_COLS)
    step = WIDTH // GRID_COLS
    dist = (x[None, :] - step * n[:, None]) % WIDTH
    base = np.ones(WIDTH)
    for kap in range(1, COL_FREQS):
        base += 2 * np.cos(2 * np.pi * ((np.arange(WIDTH) * kap) % WIDTH) / WIDTH)
    g = (base / GRID_COLS)[dist]
    g_hi, g_lo = np_split(g)
    up = np.concatenate([g_hi, g_hi, g_lo], 0)
    gt_hi, gt_lo = np_split(g.T)
    down = np.concatenate([gt_hi, gt_lo], 1)

    ang = 2 * np.pi * (np.outer(kc, n) % GRID_COLS) / GRID_COLS
    c, s = np.cos(ang) / math.sqrt(WIDTH), np.sin(ang) / math.sqrt(WIDTH)
    inv = np.block([[c, s], [-s, c]])
    i_hi, i_lo = np_split(inv)
    inv3 = np.concatenate([i_hi, i_hi, i_lo], 0)
    t_hi, t_lo = np_split(inv.T)
    adj = np.concatenate([t_hi, t_lo], 1)

    e = np.arange(SLAB)
    ang = 2 * np.pi * (np.outer(kr, e) % EXT) / EXT
    a_hi, a_lo = np_split(np.concatenate([np.cos(ang), np.sin(ang)], 0) / math.sqrt(EXT))
    lt3 = np.concatenate([a_hi, a_hi, a_lo], 1)

    m = np.arange(GRID_ROWS)
    ang = 2 * np.pi * (np.outer(m, kr) % GRID_ROWS) / GRID_ROWS
    ag = np.concatenate([np.cos(ang), np.sin(ang)], 1) / math.sqrt(EXT)
    hi, lo = np_split(ag)
    ag3 = np.concatenate([hi, hi, lo], 1)
    hi, lo = np_split(ag.T)
    agt3 = np.concatenate([hi, hi, lo], 1)

    rstep = EXT // GRID_ROWS
    dist = (e[:, None] - rstep * m[None, :]) % EXT
    base = np.ones(EXT)
    for rho in range(1, ROW_FREQS):
        base += 2 * np.cos(2 * np.pi * ((np.arange(EXT) * rho) % EXT) / EXT)
    r = (base / GRID_ROWS)[dist]
    hi, lo = np_split(r)
    r3 = np.concatenate([hi, hi, lo], 1)
    hi, lo = np_split(r.T)
    rt3 = np.concatenate([hi, hi, lo], 1)

    tabs = np.concatenate(
        [inv3, adj, pad_lanes(lt3), pad_lanes(ag3), pad_lanes(agt3), pad_lanes(r3), pad_lanes(rt3)], 0
    )

    ang = 2 * np.pi * (kr % 3) / 3
    cr = np.tile(np.cos(ang), 2)
    ci = np.tile(np.sin(ang), 2)
    with np.errstate(invalid="ignore"):
        d = np.where(kc == 0, FRAG_LEN, np.sin(np.pi * FRAG_LEN * kc / WIDTH) / np.sin(np.pi * kc / WIDTH))
    d = d / math.sqrt(WIDTH)
    col = np.concatenate([cr, ci, d, -d])
    consts = np.repeat(col[:, None], 128, 1).astype(np.float32)
    return fwd, up, down, tabs, consts


def split(x):
    hi = x.astype(BF16)
    return hi, (x - hi.astype(F32)).astype(BF16)


def dot(a, b):
    return lax.dot_general(a, b, (((1,), (0,)), ((), ())), preferred_element_type=F32)


def dot_nt(a, b):
    return lax.dot_general(a, b, (((1,), (1,)), ((), ())), preferred_element_type=F32)


def table_dot(table3, x):
    hi, lo = split(x)
    return dot(table3, jnp.concatenate([hi, lo, hi], 0))


def sin_turns(u):
    y = u * (2.0 * math.pi)
    s = y * y
    p = jnp.full_like(s, -1.0 / 39916800.0)
    for coef in (1.0 / 362880.0, -1.0 / 5040.0, 1.0 / 120.0, -1.0 / 6.0):
        p = p * s + coef
    return y + y * (s * p)


def cos_turns(t):
    t = t - jnp.floor(t + 0.5)
    return sin_turns(0.25 - jnp.abs(t))


def times_i(z, sign):
    return pltpu.roll(z, 64, axis=1) * sign


def lane_sign(shape):
    lane = lax.broadcasted_iota(jnp.int32, shape, 1)
    return jnp.where(lane < 64, -1.0, 1.0).astype(F32)


def fragment_tables(rows, cols, dsc):
    kr = lax.broadcasted_iota(jnp.int32, (32, SLOTS), 0)
    is_sin = kr >= 16
    kr = ((kr & 15) - 8).astype(F32)
    t = kr * rows.astype(F32) * (1.0 / EXT)
    row_tab = cos_turns(t - jnp.where(is_sin, 0.25, 0.0)) * (1.0 / math.sqrt(EXT))
    kc = lax.broadcasted_iota(jnp.int32, (128, SLOTS), 0)
    is_sin = kc >= 64
    kc = ((kc & 63) - 32).astype(F32)
    t = kc * (2 * cols + (FRAG_LEN - 1)).astype(F32) * (1.0 / (2 * WIDTH))
    col_tab = cos_turns(t - jnp.where(is_sin, 0.25, 0.0)) * dsc
    return row_tab, col_tab


def own_modes(packed, row_tab, col_hi, col_lo, amp, lt3, sign):
    u0 = table_dot(lt3, packed)
    hi, lo = split(row_tab * amp)
    u1 = dot_nt(
        jnp.concatenate([hi, lo, hi], 1), jnp.concatenate([col_hi, col_hi, col_lo], 1)
    )
    u_re = jnp.concatenate([u0[:16], u1[:16]], 0)
    u_im = jnp.concatenate([u0[16:], u1[16:]], 0)
    return u_re - times_i(u_im, sign)


def combine(own, left, right, cr, ci, sign):
    return own + cr * (left + right) + ci * times_i(left - right, sign)


def two_forms(h, low):
    turned = pltpu.roll(h, 64, axis=1)
    return jnp.where(low, h, turned), jnp.where(low, turned, h)


def forward_group(hrr, hii, modes, imodes, ag3, inv3):
    blocks = []
    for j in range(2):
        m, im = modes[16 * j : 16 * j + 16], imodes[16 * j : 16 * j + 16]
        for k in range(len(hrr)):
            p = hrr[k] * m + hii[k] * im
            ip = hrr[k] * im - hii[k] * m
            blocks.append(jnp.concatenate([p, ip], 0))
    rows = table_dot(ag3, jnp.concatenate(blocks, 1))
    stacked = jnp.concatenate([rows[:, 128 * b : 128 * b + 128] for b in range(len(blocks))], 0)
    hi, lo = split(stacked)
    amps = dot(jnp.concatenate([hi, lo, hi], 1), inv3)
    half = amps.shape[0] // 2
    return amps[:half], amps[half:]


def intensity_terms(e0, e1, kernels):
    total0 = total1 = None
    for k in range(kernels):
        a, b = e0[32 * k : 32 * k + 32], e1[32 * k : 32 * k + 32]
        s0, s1 = a * a, a * b
        total0 = s0 if total0 is None else total0 + s0
        total1 = s1 if total1 is None else total1 + s1
    return total0[:, :128] + total0[:, 128:], total1[:, :128] + total1[:, 128:]


def weighting(inten, change, target):
    developed = 1.0 / (1.0 + jnp.exp(-STEEP * (inten - THRESH)))
    steep = STEEP * developed * (1.0 - developed)
    return steep * (developed - target), steep * steep * change


def adjoint_group(e0, w0, w1, kernels, hrr, hii, adj, agt3):
    loads = []
    for w in (w0, w1):
        ww = jnp.concatenate([w, w], 1)
        for k in range(kernels):
            loads.append(ww * e0[32 * k : 32 * k + 32])
    hi, lo = split(jnp.concatenate(loads, 0))
    both = dot(hi, adj)
    back = both[:, :128] + both[:, 128:] + dot(lo, adj[:, :128])
    wide = jnp.concatenate([back[32 * b : 32 * b + 32] for b in range(2 * kernels)], 1)
    u = table_dot(agt3, wide)
    first, second = [], []
    for j in range(2):
        f = s = None
        for k in range(kernels):
            at = 128 * (j * kernels + k)
            u1, u2 = u[:16, at : at + 128], u[16:, at : at + 128]
            a = hrr[k] * u1 - hii[k] * u2
            b = hrr[k] * u2 + hii[k] * u1
            f = a if f is None else f + a
            s = b if s is None else s + b
        first.append(f)
        second.append(s)
    return jnp.concatenate(first, 0), jnp.concatenate(second, 0)


def project(total, row_tab, col_hi, col_lo, sign):
    it = times_i(total, sign)
    lhs = jnp.concatenate([total[:16], it[:16], total[16:], it[16:]], 0)
    hi, lo = split(lhs)
    q = dot(jnp.concatenate([hi, lo, hi], 1), jnp.concatenate([col_hi, col_hi, col_lo], 0))
    return [jnp.sum(q[32 * j : 32 * j + 32] * row_tab, axis=0, keepdims=True) for j in range(2)]


def kernel(
    weights_ref,
    counts_ref,
    rows_ref,
    cols_ref,
    step_ref,
    spectra_ref,
    tabs_ref,
    consts_ref,
    mask_hbm,
    target_hbm,
    fwd_hbm,
    up_hbm,
    down_hbm,
    grad_ref,
    curv_ref,
    mask_v,
    target_v,
    fwd_v,
    up_v,
    down_v,
    h_v,
    e0_v,
    m_own,
    m_got,
    y_own,
    y_got,
    load_sem,
    h_send,
    h_recv,
    m_send,
    m_recv,
    y_send,
    y_recv,
):
    tile = lax.axis_index("tile")
    kern = lax.axis_index("kern")
    left = lax.rem(tile + TILES - 1, TILES)
    right = lax.rem(tile + 1, TILES)
    across = lax.rem(kern + 2, KERN)
    sides = ({"tile": left, "kern": across}, {"tile": right, "kern": across})
    peers = [{"tile": tile, "kern": lax.rem(kern + d, KERN)} for d in (1, 2, 3)]

    barrier = pltpu.get_barrier_semaphore()
    for device in (*sides, *peers):
        pl.semaphore_signal(barrier, inc=1, device_id=device, device_id_type=MESH)

    width = WIDTH // CHUNKS
    mask_copies, fwd_copies = [], []
    for c in range(CHUNKS):
        part = pl.ds(c * width, width)
        mask_copies.append(
            pltpu.make_async_copy(mask_hbm.at[:, part], mask_v.at[:, part], load_sem.at[c])
        )
        fwd_copies.append(
            pltpu.make_async_copy(fwd_hbm.at[part, :], fwd_v.at[part, :], load_sem.at[CHUNKS + c])
        )
    later = [
        pltpu.make_async_copy(up_hbm, up_v, load_sem.at[2 * CHUNKS]),
        pltpu.make_async_copy(target_hbm, target_v, load_sem.at[2 * CHUNKS + 1]),
        pltpu.make_async_copy(down_hbm, down_v, load_sem.at[2 * CHUNKS + 2]),
    ]
    for a, b in zip(mask_copies, fwd_copies):
        a.start()
        b.start()
    for copy in later:
        copy.start()

    mine = pl.multiple_of(kern * LOCAL, LOCAL)
    for k in range(LOCAL):
        scale = jnp.sqrt(jnp.full((ROW_FREQS, 128), weights_ref[k] * (2.0 / KERNELS), F32))
        h_v[mine + k] = spectra_ref[k] * scale

    pl.semaphore_wait(barrier, 5)
    h_copies = []
    for d in range(3):
        copy = pltpu.make_async_remote_copy(
            src_ref=h_v.at[pl.ds(mine, LOCAL)],
            dst_ref=h_v.at[pl.ds(mine, LOCAL)],
            send_sem=h_send.at[d],
            recv_sem=h_recv.at[d],
            device_id=peers[d],
            device_id_type=MESH,
        )
        copy.start()
        h_copies.append(copy)

    sign = lane_sign((32, 128))
    cr, ci = consts_ref[0:32], consts_ref[32:64]
    dsc = consts_ref[64:192]
    row_tab, col_tab = fragment_tables(rows_ref[...], cols_ref[...], jnp.concatenate([dsc, dsc], 1))
    col_hi, col_lo = split(col_tab)
    active = lax.broadcasted_iota(jnp.int32, (1, SLOTS), 1) < counts_ref[0]
    amp = jnp.where(active, step_ref[...], 0.0) * (1.0 / math.sqrt(FRAG_LEN))

    total = jnp.zeros((2 * SLAB, 256), F32)
    for c in range(CHUNKS):
        mask_copies[c].wait()
        fwd_copies[c].wait()
        hi, lo = split(mask_v[:, c * width : (c + 1) * width])
        total += dot(jnp.concatenate([hi, lo], 0), fwd_v[c * width : (c + 1) * width, :])
    packed = total[:SLAB, :128] + total[:SLAB, 128:] + total[SLAB:, :128]
    modes_own = own_modes(packed, row_tab, col_hi, col_lo, amp, tabs_ref[640:672, :192], sign)
    m_own[...] = modes_own

    def exchange(own, got, send, recv):
        copies = []
        for d in range(2):
            copy = pltpu.make_async_remote_copy(
                src_ref=own,
                dst_ref=got.at[d],
                send_sem=send.at[d],
                recv_sem=recv.at[d],
                device_id=sides[d],
                device_id_type=MESH,
            )
            copy.start()
            copies.append(copy)
        return copies

    has_left = jnp.where(tile > 0, 1.0, 0.0).astype(F32)
    has_right = jnp.where(tile < TILES - 1, 1.0, 0.0).astype(F32)

    m_copies = exchange(m_own, m_got, m_send, m_recv)
    for copy in m_copies:
        copy.wait()
    modes = combine(modes_own, m_got[1] * has_left, m_got[0] * has_right, cr, ci, sign)
    imodes = times_i(modes, sign)

    for copy in h_copies:
        copy.wait()

    low = lax.broadcasted_iota(jnp.int32, (ROW_FREQS, 128), 1) < 64

    def forms(g):
        pairs = [two_forms(h_v[g * LOCAL + k], low) for k in range(LOCAL)]
        return [a for a, _ in pairs], [b for _, b in pairs]

    inten = change = None
    for g in range(KERN):
        hrr, hii = forms(g)
        e0, e1 = forward_group(hrr, hii, modes, imodes, tabs_ref[672:704, :96], tabs_ref[0:384, :])
        e0_v[g] = e0
        s0, s1 = intensity_terms(e0, e1, LOCAL)
        inten = s0 if inten is None else inten + s0
        change = s1 if change is None else change + s1

    grids = table_dot(tabs_ref[736:800, :96], jnp.concatenate([0.5 * inten, change], 1))
    hi, lo = split(jnp.concatenate([grids[:, :128], grids[:, 128:]], 0))
    rows3 = jnp.concatenate([hi, lo, hi], 1)
    for copy in later:
        copy.wait()
    span = 256
    total = jnp.zeros((4 * SLAB, 256), F32)
    for c in range(WIDTH // span):
        part = slice(c * span, (c + 1) * span)
        full = dot(rows3, up_v[:, part])
        w0, w1 = weighting(full[:SLAB], full[SLAB:], target_v[:, part])
        hi, lo = split(jnp.concatenate([w0, w1], 0))
        total += dot(jnp.concatenate([hi, lo], 0), down_v[part, :])
    n = 2 * SLAB
    cols = total[:n, :128] + total[:n, 128:] + total[n:, :128]
    wgrid = table_dot(tabs_ref[800:832, :192], jnp.concatenate([cols[:SLAB], cols[SLAB:]], 1))
    w0, w1 = wgrid[:, :128], wgrid[:, 128:]

    first = second = None
    for g in range(KERN):
        hrr, hii = forms(g)
        a, b = adjoint_group(
            e0_v[g], w0, w1, LOCAL, hrr, hii, tabs_ref[384:640, :], tabs_ref[704:736, :96]
        )
        first = a if first is None else first + a
        second = b if second is None else second + b
    spectrum = first - times_i(second, sign)
    y_own[...] = spectrum

    y_copies = exchange(y_own, y_got, y_send, y_recv)
    for copy in y_copies:
        copy.wait()
    whole = combine(spectrum, y_got[1] * has_left, y_got[0] * has_right, cr, ci, sign)
    outs = project(whole, row_tab, col_hi, col_lo, sign)
    for ref, out in zip((grad_ref, curv_ref), outs):
        ref[...] = jnp.where(active, out * (1.0 / math.sqrt(FRAG_LEN)), 0.0)


def shards(mask, target, spectra, weights, counts, frag_rows, frag_cols, step):
    fwd, up, down, tabs, consts = make_tables()
    vmem = pl.BlockSpec(memory_space=pltpu.VMEM)
    smem = pl.BlockSpec(memory_space=pltpu.SMEM)
    hbm = pl.BlockSpec(memory_space=pl.ANY)
    dma = pltpu.SemaphoreType.DMA
    grad, curv = pl.pallas_call(
        kernel,
        out_shape=[jax.ShapeDtypeStruct((1, SLOTS), F32)] * 2,
        in_specs=[smem, smem] + [vmem] * 6 + [hbm] * 5,
        out_specs=[vmem, vmem],
        scratch_shapes=[
            pltpu.VMEM((SLAB, WIDTH), F32),
            pltpu.VMEM((SLAB, WIDTH), F32),
            pltpu.VMEM((WIDTH, 256), BF16),
            pltpu.VMEM((384, WIDTH), BF16),
            pltpu.VMEM((WIDTH, 256), BF16),
            pltpu.VMEM((KERNELS, ROW_FREQS, 128), F32),
            pltpu.VMEM((KERN, LOCAL * GRID_ROWS, 256), F32),
            pltpu.VMEM((32, 128), F32),
            pltpu.VMEM((2, 32, 128), F32),
            pltpu.VMEM((32, 128), F32),
            pltpu.VMEM((2, 32, 128), F32),
            dma((2 * CHUNKS + 3,)),
            dma((3,)),
            dma((3,)),
            dma((2,)),
            dma((2,)),
            dma((2,)),
            dma((2,)),
        ],
        compiler_params=pltpu.CompilerParams(
            collective_id=0, has_side_effects=True, vmem_limit_bytes=48 * 1024 * 1024
        ),
    )(
        weights,
        counts,
        frag_rows.reshape(1, SLOTS),
        frag_cols.reshape(1, SLOTS),
        step.reshape(1, SLOTS),
        spectra,
        jnp.asarray(tabs),
        jnp.asarray(consts),
        mask,
        target,
        jnp.asarray(fwd),
        jnp.asarray(up),
        jnp.asarray(down),
    )
    return grad.reshape(SLOTS), curv.reshape(SLOTS)


def solution(mesh):
    return jax.shard_map(
        shards,
        mesh=mesh,
        in_specs=(
            P("tile", None),
            P("tile", None),
            P("kern", None, None),
            P("kern"),
            P("tile"),
            P("tile"),
            P("tile"),
            P("tile"),
        ),
        out_specs=(P("tile"), P("tile")),
        check_vma=False,
    )
```

profile of v0, /device:TPU:1, one launch (start us, length us, event | category | flops | bytes accessed | tf_op | source)
XLA Modules:
  0.0 39.9 jit_solution(3724546896666941210)
XLA Ops:
  1.3 0.0 copy-start
  1.3 1.4 %copy-done = bf16[384,2048]{1,0:T(8,128)(2,1)S(1)} copy-done((bf16[384,2048]{1,0:T(8,128)(2,1)S(1)}, bf16[384,2048]{1,0:T(8,128)(2,1)}, u32[]{:S(2)}) %copy-start) | copy-done | bytes 1572888
  2.7 0.0 copy-start.1
  2.7 1.2 %copy-done.1 = bf16[2048,256]{1,0:T(8,128)(2,1)S(1)} copy-done((bf16[2048,256]{1,0:T(8,128)(2,1)S(1)}, bf16[2048,256]{1,0:T(8,128)(2,1)}, u32[]{:S(2)}) %copy-start.1) | copy-done | bytes 1048600
  3.9 0.0 copy-start.2
  3.9 1.2 %copy-done.2 = bf16[2048,256]{1,0:T(8,128)(2,1)S(1)} copy-done((bf16[2048,256]{1,0:T(8,128)(2,1)S(1)}, bf16[2048,256]{1,0:T(8,128)(2,1)}, u32[]{:S(2)}) %copy-start.2) | copy-done | bytes 1048600
  5.1 0.0 copy-start.3
  5.1 1.0 %copy-done.3 = f32[64,2048]{1,0:T(8,128)S(1)} copy-done((f32[64,2048]{1,0:T(8,128)S(1)}, f32[64,2048]{1,0:T(8,128)}, u32[]{:S(2)}) %copy-start.3) | copy-done | bytes 524312
  6.2 0.0 copy-start.4
  6.2 1.0 %copy-done.4 = f32[64,2048]{1,0:T(8,128)S(1)} copy-done((f32[64,2048]{1,0:T(8,128)S(1)}, f32[64,2048]{1,0:T(8,128)}, u32[]{:S(2)}) %copy-start.4) | copy-done | bytes 524312
  7.2 0.0 copy-start.5
  7.2 1.0 %copy-done.5 = bf16[832,256]{1,0:T(8,128)(2,1)S(1)} copy-done((bf16[832,256]{1,0:T(8,128)(2,1)S(1)}, bf16[832,256]{1,0:T(8,128)(2,1)}, u32[]{:S(2)}) %copy-start.5) | copy-done | bytes 426008
  8.2 0.0 copy-start.6
  8.2 0.9 %copy-done.6 = f32[192,128]{1,0:T(8,128)S(1)} copy-done((f32[192,128]{1,0:T(8,128)S(1)}, f32[192,128]{1,0:T(8,128)}, u32[]{:S(2)}) %copy-start.6) | copy-done | bytes 98328
  9.1 0.0 copy-start.7
  9.1 0.8 %copy-done.7 = f32[6,16,128]{2,1,0:T(8,128)S(1)} copy-done((f32[6,16,128]{2,1,0:T(8,128)S(1)}, f32[6,16,128]{2,1,0:T(8,128)}, u32[]{:S(2)}) %copy-start.7) | copy-done | bytes 49176
  9.9 0.0 copy-start.8
  9.9 0.7 %copy-done.8 = s32[256]{0:T(256)S(1)} copy-done((s32[256]{0:T(256)S(1)}, s32[256]{0:T(256)}, u32[]{:S(2)}) %copy-start.8) | copy-done | bytes 1048
  10.6 0.7 %copy-done.9 = s32[256]{0:T(256)S(1)} copy-done((s32[256]{0:T(256)S(1)}, s32[256]{0:T(256)}, u32[]{:S(2)}) %copy-start.9) | copy-done | bytes 1048
  11.3 0.7 %copy-done.10 = f32[256]{0:T(256)S(1)} copy-done((f32[256]{0:T(256)S(1)}, f32[256]{0:T(256)}, u32[]{:S(2)}) %copy-start.10) | copy-done | bytes 1048
  12.0 0.7 %copy-done.11 = f32[6]{0:T(128)S(1)} copy-done((f32[6]{0:T(128)S(1)}, f32[6]{0:T(128)}, u32[]{:S(2)}) %copy-start.11) | copy-done | bytes 48
  12.6 26.1 %shard_map.140 = (f32[1,256]{1,0:T(1,128)S(1)}, f32[1,256]{1,0:T(1,128)S(1)}) custom-call(f32[6]{0:T(128)S(1)} %copy-done.11, s32[1]{0:T(128)S(6)} %copy.17.counts_ref, s32[1,256]{1,0:T(1,128)S(1)} %bitcast.5, s32[1,256]{1,0:T(1,128)S(1)} %bitcast.6, f32[1,256]{1,0:T(1,128)S(1)} %bitcast.7, f32[6,16,128]{2,1,0:T(8,128)S(1)} %copy-done.7, ...), custom_call_target="tpu_custom_call" | custom-call | tf_op jit(solution)/shard_map/pallas_call | solution.py:444
  38.7 0.6 %copy.18 = f32[256]{0:T(256)} copy(f32[256]{0:T(256)S(1)} %bitcast.9) | data formatting | bytes 2048
  39.3 0.6 %copy.19 = f32[256]{0:T(256)} copy(f32[256]{0:T(256)S(1)} %bitcast.8) | data formatting | bytes 2048
  (3 shorter events, 0.0 us)
Async XLA Ops:
  1.3 1.4 %copy-start = (bf16[384,2048]{1,0:T(8,128)(2,1)S(1)}, bf16[384,2048]{1,0:T(8,128)(2,1)}, u32[]{:S(2)}) copy-start(bf16[384,2048]{1,0:T(8,128)(2,1)} %constant.13.clone.up_hbm) | copy-start | bytes 4718596
  2.7 1.2 %copy-start.1 = (bf16[2048,256]{1,0:T(8,128)(2,1)S(1)}, bf16[2048,256]{1,0:T(8,128)(2,1)}, u32[]{:S(2)}) copy-start(bf16[2048,256]{1,0:T(8,128)(2,1)} %constant.14.clone.down_hbm) | copy-start | bytes 3145732
  3.9 1.2 %copy-start.2 = (bf16[2048,256]{1,0:T(8,128)(2,1)S(1)}, bf16[2048,256]{1,0:T(8,128)(2,1)}, u32[]{:S(2)}) copy-start(bf16[2048,256]{1,0:T(8,128)(2,1)} %constant.12.clone.fwd_hbm) | copy-start | bytes 3145732
  5.1 1.0 %copy-start.3 = (f32[64,2048]{1,0:T(8,128)S(1)}, f32[64,2048]{1,0:T(8,128)}, u32[]{:S(2)}) copy-start(f32[64,2048]{1,0:T(8,128)} %mask_hbm.1) | copy-start | bytes 1572868
  6.2 1.0 %copy-start.4 = (f32[64,2048]{1,0:T(8,128)S(1)}, f32[64,2048]{1,0:T(8,128)}, u32[]{:S(2)}) copy-start(f32[64,2048]{1,0:T(8,128)} %target_hbm.1) | copy-start | bytes 1572868
  7.2 1.0 %copy-start.5 = (bf16[832,256]{1,0:T(8,128)(2,1)S(1)}, bf16[832,256]{1,0:T(8,128)(2,1)}, u32[]{:S(2)}) copy-start(bf16[832,256]{1,0:T(8,128)(2,1)} %constant.10.clone.tabs_ref) | copy-start | bytes 1277956
  8.2 0.9 %copy-start.6 = (f32[192,128]{1,0:T(8,128)S(1)}, f32[192,128]{1,0:T(8,128)}, u32[]{:S(2)}) copy-start(f32[192,128]{1,0:T(8,128)} %constant.11.clone.consts_ref) | copy-start | bytes 294916
  9.1 0.8 %copy-start.7 = (f32[6,16,128]{2,1,0:T(8,128)S(1)}, f32[6,16,128]{2,1,0:T(8,128)}, u32[]{:S(2)}) copy-start(f32[6,16,128]{2,1,0:T(8,128)} %spectra_ref.1) | copy-start | bytes 147460
  9.9 0.7 %copy-start.8 = (s32[256]{0:T(256)S(1)}, s32[256]{0:T(256)}, u32[]{:S(2)}) copy-start(s32[256]{0:T(256)} %param.18) | copy-start | bytes 3076
  10.6 0.7 %copy-start.9 = (s32[256]{0:T(256)S(1)}, s32[256]{0:T(256)}, u32[]{:S(2)}) copy-start(s32[256]{0:T(256)} %param.19) | copy-start | bytes 3076
  11.3 0.7 %copy-start.10 = (f32[256]{0:T(256)S(1)}, f32[256]{0:T(256)}, u32[]{:S(2)}) copy-start(f32[256]{0:T(256)} %param.20) | copy-start | bytes 3076
  12.0 0.7 %copy-start.11 = (f32[6]{0:T(128)S(1)}, f32[6]{0:T(128)}, u32[]{:S(2)}) copy-start(f32[6]{0:T(128)} %weights_ref.1) | copy-start | bytes 76
where the time goes:
time: 40.3 us; the launch traced here: 39.9 us
  Pallas kernels  26.1 us (65%)
  local copies, waits for them, and re-layouts  12.4 us (31%)
  between operations  1.31 us (3%)
    pallas_call x1, Pallas kernels, shards(): pl.pallas_call(kernel, out_shape=[jax.ShapeDtypeStruct((1, SLOTS), F32)]...  26.1 us
    unnamed x26, local copies, waits for them, and re-layouts  12.4 us

commit v1 on v0

--- a/solution.py
+++ b/solution.py
@@ -251,21 +251,28 @@
 
 
 def kernel(
-    weights_ref,
-    counts_ref,
-    rows_ref,
-    cols_ref,
-    step_ref,
-    spectra_ref,
-    tabs_ref,
-    consts_ref,
+    weights_hbm,
+    counts_hbm,
+    rows_hbm,
+    cols_hbm,
+    step_hbm,
+    spectra_hbm,
+    tabs_hbm,
+    consts_hbm,
     mask_hbm,
     target_hbm,
     fwd_hbm,
     up_hbm,
     down_hbm,
-    grad_ref,
-    curv_ref,
+    out_ref,
+    weights_s,
+    counts_s,
+    rows_v,
+    cols_v,
+    step_v,
+    spectra_v,
+    tabs_v,
+    consts_v,
     mask_v,
     target_v,
     fwd_v,
@@ -287,43 +294,69 @@
 ):
     tile = lax.axis_index("tile")
     kern = lax.axis_index("kern")
-    left = lax.rem(tile + TILES - 1, TILES)
-    right = lax.rem(tile + 1, TILES)
     across = lax.rem(kern + 2, KERN)
-    sides = ({"tile": left, "kern": across}, {"tile": right, "kern": across})
+    sides = (
+        (tile > 0, {"tile": lax.max(tile - 1, 0), "kern": across}),
+        (tile < TILES - 1, {"tile": lax.min(tile + 1, TILES - 1), "kern": across}),
+    )
     peers = [{"tile": tile, "kern": lax.rem(kern + d, KERN)} for d in (1, 2, 3)]
 
+    for d, (exists, _) in enumerate(sides):
+
+        @pl.when(jnp.logical_not(exists))
+        def _():
+            m_got[1 - d] = jnp.zeros((32, 128), F32)
+            y_got[1 - d] = jnp.zeros((32, 128), F32)
+
     barrier = pltpu.get_barrier_semaphore()
-    for device in (*sides, *peers):
+    for device in peers:
         pl.semaphore_signal(barrier, inc=1, device_id=device, device_id_type=MESH)
+    for exists, device in sides:
+
+        @pl.when(exists)
+        def _():
+            pl.semaphore_signal(barrier, inc=1, device_id=device, device_id_type=MESH)
+
+    used = []
+
+    def load(src, dst):
+        copy = pltpu.make_async_copy(src, dst, load_sem.at[len(used)])
+        used.append(copy)
+        return copy
 
     width = WIDTH // CHUNKS
-    mask_copies, fwd_copies = [], []
-    for c in range(CHUNKS):
-        part = pl.ds(c * width, width)
-        mask_copies.append(
-            pltpu.make_async_copy(mask_hbm.at[:, part], mask_v.at[:, part], load_sem.at[c])
+    early = [load(weights_hbm, weights_s), load(spectra_hbm, spectra_v)]
+    small = [
+        load(a, b)
+        for a, b in (
+            (counts_hbm, counts_s),
+            (rows_hbm, rows_v),
+            (cols_hbm, cols_v),
+            (step_hbm, step_v),
+            (consts_hbm, consts_v),
+            (tabs_hbm, tabs_v),
         )
-        fwd_copies.append(
-            pltpu.make_async_copy(fwd_hbm.at[part, :], fwd_v.at[part, :], load_sem.at[CHUNKS + c])
-        )
-    later = [
-        pltpu.make_async_copy(up_hbm, up_v, load_sem.at[2 * CHUNKS]),
-        pltpu.make_async_copy(target_hbm, target_v, load_sem.at[2 * CHUNKS + 1]),
-        pltpu.make_async_copy(down_hbm, down_v, load_sem.at[2 * CHUNKS + 2]),
     ]
+    parts = [pl.ds(c * width, width) for c in range(CHUNKS)]
+    mask_copies = [load(mask_hbm.at[:, p], mask_v.at[:, p]) for p in parts]
+    fwd_copies = [load(fwd_hbm.at[p, :], fwd_v.at[p, :]) for p in parts]
+    later = [load(up_hbm, up_v), load(target_hbm, target_v), load(down_hbm, down_v)]
+    for copy in early:
+        copy.start()
     for a, b in zip(mask_copies, fwd_copies):
         a.start()
         b.start()
-    for copy in later:
+    for copy in small + later:
         copy.start()
 
+    for copy in early:
+        copy.wait()
     mine = pl.multiple_of(kern * LOCAL, LOCAL)
     for k in range(LOCAL):
-        scale = jnp.sqrt(jnp.full((ROW_FREQS, 128), weights_ref[k] * (2.0 / KERNELS), F32))
-        h_v[mine + k] = spectra_ref[k] * scale
-
-    pl.semaphore_wait(barrier, 5)
+        scale = jnp.sqrt(jnp.full((ROW_FREQS, 128), weights_s[k] * (2.0 / KERNELS), F32))
+        h_v[mine + k] = spectra_v[k] * scale
+
+    pl.semaphore_wait(barrier, 3 + lax.min(tile, 1) + lax.min(TILES - 1 - tile, 1))
     h_copies = []
     for d in range(3):
         copy = pltpu.make_async_remote_copy(
@@ -337,13 +370,15 @@
         copy.start()
         h_copies.append(copy)
 
+    for copy in small:
+        copy.wait()
     sign = lane_sign((32, 128))
-    cr, ci = consts_ref[0:32], consts_ref[32:64]
-    dsc = consts_ref[64:192]
-    row_tab, col_tab = fragment_tables(rows_ref[...], cols_ref[...], jnp.concatenate([dsc, dsc], 1))
+    cr, ci = consts_v[0:32], consts_v[32:64]
+    dsc = consts_v[64:192]
+    row_tab, col_tab = fragment_tables(rows_v[...], cols_v[...], jnp.concatenate([dsc, dsc], 1))
     col_hi, col_lo = split(col_tab)
-    active = lax.broadcasted_iota(jnp.int32, (1, SLOTS), 1) < counts_ref[0]
-    amp = jnp.where(active, step_ref[...], 0.0) * (1.0 / math.sqrt(FRAG_LEN))
+    active = lax.broadcasted_iota(jnp.int32, (1, SLOTS), 1) < counts_s[0]
+    amp = jnp.where(active, step_v[...], 0.0) * (1.0 / math.sqrt(FRAG_LEN))
 
     total = jnp.zeros((2 * SLAB, 256), F32)
     for c in range(CHUNKS):
@@ -352,31 +387,44 @@
         hi, lo = split(mask_v[:, c * width : (c + 1) * width])
         total += dot(jnp.concatenate([hi, lo], 0), fwd_v[c * width : (c + 1) * width, :])
     packed = total[:SLAB, :128] + total[:SLAB, 128:] + total[SLAB:, :128]
-    modes_own = own_modes(packed, row_tab, col_hi, col_lo, amp, tabs_ref[640:672, :192], sign)
+    modes_own = own_modes(packed, row_tab, col_hi, col_lo, amp, tabs_v[640:672, :192], sign)
     m_own[...] = modes_own
 
     def exchange(own, got, send, recv):
-        copies = []
-        for d in range(2):
-            copy = pltpu.make_async_remote_copy(
+        copies = [
+            pltpu.make_async_remote_copy(
                 src_ref=own,
                 dst_ref=got.at[d],
                 send_sem=send.at[d],
                 recv_sem=recv.at[d],
-                device_id=sides[d],
+                device_id=device,
                 device_id_type=MESH,
             )
-            copy.start()
-            copies.append(copy)
+            for d, (_, device) in enumerate(sides)
+        ]
+        for d, (exists, _) in enumerate(sides):
+
+            @pl.when(exists)
+            def _():
+                copies[d].start()
+
+        for d, (exists, _) in enumerate(sides):
+
+            @pl.when(exists)
+            def _():
+                copies[1 - d].wait_recv()
+
         return copies
 
-    has_left = jnp.where(tile > 0, 1.0, 0.0).astype(F32)
-    has_right = jnp.where(tile < TILES - 1, 1.0, 0.0).astype(F32)
+    def sent(copies):
+        for d, (exists, _) in enumerate(sides):
+
+            @pl.when(exists)
+            def _():
+                copies[d].wait_send()
 
     m_copies = exchange(m_own, m_got, m_send, m_recv)
-    for copy in m_copies:
-        copy.wait()
-    modes = combine(modes_own, m_got[1] * has_left, m_got[0] * has_right, cr, ci, sign)
+    modes = combine(modes_own, m_got[1], m_got[0], cr, ci, sign)
     imodes = times_i(modes, sign)
 
     for copy in h_copies:
@@ -391,13 +439,13 @@
     inten = change = None
     for g in range(KERN):
         hrr, hii = forms(g)
-        e0, e1 = forward_group(hrr, hii, modes, imodes, tabs_ref[672:704, :96], tabs_ref[0:384, :])
+        e0, e1 = forward_group(hrr, hii, modes, imodes, tabs_v[672:704, :96], tabs_v[0:384, :])
         e0_v[g] = e0
         s0, s1 = intensity_terms(e0, e1, LOCAL)
         inten = s0 if inten is None else inten + s0
         change = s1 if change is None else change + s1
 
-    grids = table_dot(tabs_ref[736:800, :96], jnp.concatenate([0.5 * inten, change], 1))
+    grids = table_dot(tabs_v[736:800, :96], jnp.concatenate([0.5 * inten, change], 1))
     hi, lo = split(jnp.concatenate([grids[:, :128], grids[:, 128:]], 0))
     rows3 = jnp.concatenate([hi, lo, hi], 1)
     for copy in later:
@@ -412,14 +460,14 @@
         total += dot(jnp.concatenate([hi, lo], 0), down_v[part, :])
     n = 2 * SLAB
     cols = total[:n, :128] + total[:n, 128:] + total[n:, :128]
-    wgrid = table_dot(tabs_ref[800:832, :192], jnp.concatenate([cols[:SLAB], cols[SLAB:]], 1))
+    wgrid = table_dot(tabs_v[800:832, :192], jnp.concatenate([cols[:SLAB], cols[SLAB:]], 1))
     w0, w1 = wgrid[:, :128], wgrid[:, 128:]
 
     first = second = None
     for g in range(KERN):
         hrr, hii = forms(g)
         a, b = adjoint_group(
-            e0_v[g], w0, w1, LOCAL, hrr, hii, tabs_ref[384:640, :], tabs_ref[704:736, :96]
+            e0_v[g], w0, w1, LOCAL, hrr, hii, tabs_v[384:640, :], tabs_v[704:736, :96]
         )
         first = a if first is None else first + a
         second = b if second is None else second + b
@@ -427,26 +475,33 @@
     y_own[...] = spectrum
 
     y_copies = exchange(y_own, y_got, y_send, y_recv)
-    for copy in y_copies:
-        copy.wait()
-    whole = combine(spectrum, y_got[1] * has_left, y_got[0] * has_right, cr, ci, sign)
+    whole = combine(spectrum, y_got[1], y_got[0], cr, ci, sign)
     outs = project(whole, row_tab, col_hi, col_lo, sign)
-    for ref, out in zip((grad_ref, curv_ref), outs):
-        ref[...] = jnp.where(active, out * (1.0 / math.sqrt(FRAG_LEN)), 0.0)
+    for j in range(2):
+        out_ref[j : j + 1, :] = jnp.where(active, outs[j] * (1.0 / math.sqrt(FRAG_LEN)), 0.0)
+    sent(m_copies)
+    sent(y_copies)
 
 
 def shards(mask, target, spectra, weights, counts, frag_rows, frag_cols, step):
     fwd, up, down, tabs, consts = make_tables()
     vmem = pl.BlockSpec(memory_space=pltpu.VMEM)
-    smem = pl.BlockSpec(memory_space=pltpu.SMEM)
-    hbm = pl.BlockSpec(memory_space=pl.ANY)
+    hbm = pl.BlockSpec(memory_space=pltpu.HBM)
     dma = pltpu.SemaphoreType.DMA
-    grad, curv = pl.pallas_call(
+    outs = pl.pallas_call(
         kernel,
-        out_shape=[jax.ShapeDtypeStruct((1, SLOTS), F32)] * 2,
-        in_specs=[smem, smem] + [vmem] * 6 + [hbm] * 5,
-        out_specs=[vmem, vmem],
+        out_shape=jax.ShapeDtypeStruct((2, SLOTS), F32),
+        in_specs=[hbm] * 13,
+        out_specs=vmem,
         scratch_shapes=[
+            pltpu.SMEM((LOCAL,), F32),
+            pltpu.SMEM((1,), jnp.int32),
+            pltpu.VMEM((1, SLOTS), jnp.int32),
+            pltpu.VMEM((1, SLOTS), jnp.int32),
+            pltpu.VMEM((1, SLOTS), F32),
+            pltpu.VMEM((LOCAL, ROW_FREQS, 128), F32),
+            pltpu.VMEM(tabs.shape, BF16),
+            pltpu.VMEM(consts.shape, F32),
             pltpu.VMEM((SLAB, WIDTH), F32),
             pltpu.VMEM((SLAB, WIDTH), F32),
             pltpu.VMEM((WIDTH, 256), BF16),
@@ -458,7 +513,7 @@
             pltpu.VMEM((2, 32, 128), F32),
             pltpu.VMEM((32, 128), F32),
             pltpu.VMEM((2, 32, 128), F32),
-            dma((2 * CHUNKS + 3,)),
+            dma((2 * CHUNKS + 11,)),
             dma((3,)),
             dma((3,)),
             dma((2,)),
@@ -467,7 +522,7 @@
             dma((2,)),
         ],
         compiler_params=pltpu.CompilerParams(
-            collective_id=0, has_side_effects=True, vmem_limit_bytes=48 * 1024 * 1024
+            collective_id=0, has_side_effects=True, vmem_limit_bytes=64 * 1024 * 1024
         ),
     )(
         weights,
@@ -484,7 +539,7 @@
         jnp.asarray(up),
         jnp.asarray(down),
     )
-    return grad.reshape(SLOTS), curv.reshape(SLOTS)
+    return outs[0], outs[1]
 
 
 def solution(mesh):

time: 40.3 us -> 27.2 us (0.67)
  the two profiles are of different devices: /device:TPU:1 before, /device:TPU:6 now
where the time goes in v1:
time: 27.2 us; the launch traced here: 27.1 us
  Pallas kernels  24.5 us (90%)
  local copies, waits for them, and re-layouts  1.32 us (5%)
  between operations  1.29 us (5%)
    pallas_call x1, Pallas kernels, shards(): pl.pallas_call(kernel, out_shape=jax.ShapeDtypeStruct((2, SLOTS), F32), i...  24.5 us
    slice x1, local copies, waits for them, and re-layouts, shards(): return (outs[0], outs[1])  1.32 us

profile of v1, /device:TPU:6, one launch (start us, length us, event | category | flops | bytes accessed | tf_op | source)
XLA Modules:
  0.0 27.1 jit_solution(2991498083146148580)
XLA Ops:
  1.3 24.5 %shard_map.140 = f32[2,256]{1,0:T(2,128)} custom-call(f32[6]{0:T(128)} %weights_hbm.1, s32[1]{0:T(128)S(6)} %copy.15.counts_hbm, s32[1,256]{1,0:T(1,128)} %bitcast.7, s32[1,256]{1,0:T(1,128)} %bitcast.8, f32[1,256]{1,0:T(1,128)} %bitcast.9, f32[6,16,128]{2,1,0:T(8,128)} %spectra_hbm.1, bf16[832,256]{1,0:T(8,128)(2,1)} %constant.10.clone.tabs_hbm, ...), custom_call_target="tpu_custom_call" | custom-call | tf_op jit(solution)/shard_map/pallas_call | solution.py:491
  25.8 1.3 %fusion = (f32[1,256]{1,0:T(1,128)}, f32[1,256]{1,0:T(1,128)}) fusion(f32[2,256]{1,0:T(2,128)} %shard_map.140), kind=kLoop, calls=%fused_computation | loop fusion | bytes 4096 | tf_op jit(solution)/shard_map/slice | solution.py:542

commit v2 on v1

--- a/solution.py
+++ b/solution.py
@@ -284,6 +284,9 @@
     m_got,
     y_own,
     y_got,
+    hrr_v,
+    hii_v,
+    res_v,
     load_sem,
     h_send,
     h_recv,
@@ -291,32 +294,19 @@
     m_recv,
     y_send,
     y_recv,
+    res_send,
+    res_recv,
 ):
     tile = lax.axis_index("tile")
     kern = lax.axis_index("kern")
-    across = lax.rem(kern + 2, KERN)
+    lead = 3 - 2 * lax.rem(tile, 2)
+    is_lead = kern == lead
+    others = [{"tile": tile, "kern": lax.rem(lead + d, KERN)} for d in (1, 2, 3)]
     sides = (
-        (tile > 0, {"tile": lax.max(tile - 1, 0), "kern": across}),
-        (tile < TILES - 1, {"tile": lax.min(tile + 1, TILES - 1), "kern": across}),
+        (tile > 0, {"tile": lax.max(tile - 1, 0), "kern": 4 - lead}),
+        (tile < TILES - 1, {"tile": lax.min(tile + 1, TILES - 1), "kern": 4 - lead}),
     )
-    peers = [{"tile": tile, "kern": lax.rem(kern + d, KERN)} for d in (1, 2, 3)]
-
-    for d, (exists, _) in enumerate(sides):
-
-        @pl.when(jnp.logical_not(exists))
-        def _():
-            m_got[1 - d] = jnp.zeros((32, 128), F32)
-            y_got[1 - d] = jnp.zeros((32, 128), F32)
-
     barrier = pltpu.get_barrier_semaphore()
-    for device in peers:
-        pl.semaphore_signal(barrier, inc=1, device_id=device, device_id_type=MESH)
-    for exists, device in sides:
-
-        @pl.when(exists)
-        def _():
-            pl.semaphore_signal(barrier, inc=1, device_id=device, device_id_type=MESH)
-
     used = []
 
     def load(src, dst):
@@ -324,163 +314,231 @@
         used.append(copy)
         return copy
 
-    width = WIDTH // CHUNKS
     early = [load(weights_hbm, weights_s), load(spectra_hbm, spectra_v)]
-    small = [
-        load(a, b)
-        for a, b in (
-            (counts_hbm, counts_s),
-            (rows_hbm, rows_v),
-            (cols_hbm, cols_v),
-            (step_hbm, step_v),
-            (consts_hbm, consts_v),
-            (tabs_hbm, tabs_v),
-        )
-    ]
-    parts = [pl.ds(c * width, width) for c in range(CHUNKS)]
-    mask_copies = [load(mask_hbm.at[:, p], mask_v.at[:, p]) for p in parts]
-    fwd_copies = [load(fwd_hbm.at[p, :], fwd_v.at[p, :]) for p in parts]
-    later = [load(up_hbm, up_v), load(target_hbm, target_v), load(down_hbm, down_v)]
-    for copy in early:
-        copy.start()
-    for a, b in zip(mask_copies, fwd_copies):
-        a.start()
-        b.start()
-    for copy in small + later:
-        copy.start()
-
-    for copy in early:
-        copy.wait()
     mine = pl.multiple_of(kern * LOCAL, LOCAL)
-    for k in range(LOCAL):
-        scale = jnp.sqrt(jnp.full((ROW_FREQS, 128), weights_s[k] * (2.0 / KERNELS), F32))
-        h_v[mine + k] = spectra_v[k] * scale
-
-    pl.semaphore_wait(barrier, 3 + lax.min(tile, 1) + lax.min(TILES - 1 - tile, 1))
-    h_copies = []
-    for d in range(3):
+
+    def scale_own():
+        for copy in early:
+            copy.wait()
+        for k in range(LOCAL):
+            scale = jnp.sqrt(jnp.full((ROW_FREQS, 128), weights_s[k] * (2.0 / KERNELS), F32))
+            h_v[mine + k] = spectra_v[k] * scale
+
+    @pl.when(jnp.logical_not(is_lead))
+    def _():
+        lead_device = {"tile": tile, "kern": lead}
+        pl.semaphore_signal(barrier, inc=1, device_id=lead_device, device_id_type=MESH)
+        for copy in early:
+            copy.start()
+        scale_own()
+        pl.semaphore_wait(barrier, 1)
+        place = lax.rem(kern - lead + KERN, KERN) - 1
         copy = pltpu.make_async_remote_copy(
             src_ref=h_v.at[pl.ds(mine, LOCAL)],
             dst_ref=h_v.at[pl.ds(mine, LOCAL)],
-            send_sem=h_send.at[d],
-            recv_sem=h_recv.at[d],
-            device_id=peers[d],
+            send_sem=h_send.at[0],
+            recv_sem=h_recv.at[place],
+            device_id=lead_device,
             device_id_type=MESH,
         )
         copy.start()
-        h_copies.append(copy)
-
-    for copy in small:
-        copy.wait()
-    sign = lane_sign((32, 128))
-    cr, ci = consts_v[0:32], consts_v[32:64]
-    dsc = consts_v[64:192]
-    row_tab, col_tab = fragment_tables(rows_v[...], cols_v[...], jnp.concatenate([dsc, dsc], 1))
-    col_hi, col_lo = split(col_tab)
-    active = lax.broadcasted_iota(jnp.int32, (1, SLOTS), 1) < counts_s[0]
-    amp = jnp.where(active, step_v[...], 0.0) * (1.0 / math.sqrt(FRAG_LEN))
-
-    total = jnp.zeros((2 * SLAB, 256), F32)
-    for c in range(CHUNKS):
-        mask_copies[c].wait()
-        fwd_copies[c].wait()
-        hi, lo = split(mask_v[:, c * width : (c + 1) * width])
-        total += dot(jnp.concatenate([hi, lo], 0), fwd_v[c * width : (c + 1) * width, :])
-    packed = total[:SLAB, :128] + total[:SLAB, 128:] + total[SLAB:, :128]
-    modes_own = own_modes(packed, row_tab, col_hi, col_lo, amp, tabs_v[640:672, :192], sign)
-    m_own[...] = modes_own
-
-    def exchange(own, got, send, recv):
-        copies = [
+        copy.wait_send()
+        pltpu.make_async_remote_copy(
+            src_ref=res_v,
+            dst_ref=res_v,
+            send_sem=res_send.at[0],
+            recv_sem=res_recv.at[0],
+            device_id=lead_device,
+            device_id_type=MESH,
+        ).wait_recv()
+
+    @pl.when(is_lead)
+    def _():
+        for d, (exists, _) in enumerate(sides):
+
+            @pl.when(jnp.logical_not(exists))
+            def _():
+                m_got[1 - d] = jnp.zeros((32, 128), F32)
+                y_got[1 - d] = jnp.zeros((32, 128), F32)
+
+        for exists, device in sides:
+
+            @pl.when(exists)
+            def _():
+                pl.semaphore_signal(barrier, inc=1, device_id=device, device_id_type=MESH)
+
+        for device in others:
+            pl.semaphore_signal(barrier, inc=1, device_id=device, device_id_type=MESH)
+
+        width = WIDTH // CHUNKS
+        small = [
+            load(a, b)
+            for a, b in (
+                (counts_hbm, counts_s),
+                (rows_hbm, rows_v),
+                (cols_hbm, cols_v),
+                (step_hbm, step_v),
+                (consts_hbm, consts_v),
+                (tabs_hbm, tabs_v),
+            )
+        ]
+        parts = [pl.ds(c * width, width) for c in range(CHUNKS)]
+        mask_copies = [load(mask_hbm.at[:, p], mask_v.at[:, p]) for p in parts]
+        fwd_copies = [load(fwd_hbm.at[p, :], fwd_v.at[p, :]) for p in parts]
+        later = [load(up_hbm, up_v), load(target_hbm, target_v), load(down_hbm, down_v)]
+        for a, b in zip(mask_copies, fwd_copies):
+            a.start()
+            b.start()
+        for copy in early + small + later:
+            copy.start()
+
+        for copy in small:
+            copy.wait()
+        sign = lane_sign((32, 128))
+        cr, ci = consts_v[0:32], consts_v[32:64]
+        dsc = consts_v[64:192]
+        row_tab, col_tab = fragment_tables(rows_v[...], cols_v[...], jnp.concatenate([dsc, dsc], 1))
+        col_hi, col_lo = split(col_tab)
+        active = lax.broadcasted_iota(jnp.int32, (1, SLOTS), 1) < counts_s[0]
+        amp = jnp.where(active, step_v[...], 0.0) * (1.0 / math.sqrt(FRAG_LEN))
+
+        total = jnp.zeros((2 * SLAB, 256), F32)
+        for c in range(CHUNKS):
+            mask_copies[c].wait()
+            fwd_copies[c].wait()
+            hi, lo = split(mask_v[:, c * width : (c + 1) * width])
+            total += dot(jnp.concatenate([hi, lo], 0), fwd_v[c * width : (c + 1) * width, :])
+        packed = total[:SLAB, :128] + total[:SLAB, 128:] + total[SLAB:, :128]
+        modes_own = own_modes(packed, row_tab, col_hi, col_lo, amp, tabs_v[640:672, :192], sign)
+        m_own[...] = modes_own
+
+        def exchange(own, got, send, recv):
+            copies = [
+                pltpu.make_async_remote_copy(
+                    src_ref=own,
+                    dst_ref=got.at[d],
+                    send_sem=send.at[d],
+                    recv_sem=recv.at[d],
+                    device_id=device,
+                    device_id_type=MESH,
+                )
+                for d, (_, device) in enumerate(sides)
+            ]
+            for d, (exists, _) in enumerate(sides):
+
+                @pl.when(exists)
+                def _():
+                    copies[d].start()
+
+            return copies
+
+        def arrived(copies):
+            for d, (exists, _) in enumerate(sides):
+
+                @pl.when(exists)
+                def _():
+                    copies[1 - d].wait_recv()
+
+        def sent(copies):
+            for d, (exists, _) in enumerate(sides):
+
+                @pl.when(exists)
+                def _():
+                    copies[d].wait_send()
+
+        pl.semaphore_wait(barrier, 3 + lax.min(tile, 1) + lax.min(TILES - 1 - tile, 1))
+        m_copies = exchange(m_own, m_got, m_send, m_recv)
+
+        scale_own()
+        low = lax.broadcasted_iota(jnp.int32, (ROW_FREQS, 128), 1) < 64
+        for d in range(KERN):
+            at = pl.multiple_of(lax.rem(lead + d, KERN) * LOCAL, LOCAL)
+            if d > 0:
+                pltpu.make_async_remote_copy(
+                    src_ref=h_v.at[pl.ds(at, LOCAL)],
+                    dst_ref=h_v.at[pl.ds(at, LOCAL)],
+                    send_sem=h_send.at[0],
+                    recv_sem=h_recv.at[d - 1],
+                    device_id=others[0],
+                    device_id_type=MESH,
+                ).wait_recv()
+            for k in range(LOCAL):
+                a, b = two_forms(h_v[at + k], low)
+                hrr_v[d * LOCAL + k] = a
+                hii_v[d * LOCAL + k] = b
+
+        def forms(g):
+            ks = range(g * LOCAL, (g + 1) * LOCAL)
+            return [hrr_v[k] for k in ks], [hii_v[k] for k in ks]
+
+        for copy in later:
+            copy.wait()
+        arrived(m_copies)
+        modes = combine(modes_own, m_got[1], m_got[0], cr, ci, sign)
+        imodes = times_i(modes, sign)
+
+        inten = change = None
+        for g in range(KERN):
+            hrr, hii = forms(g)
+            e0, e1 = forward_group(hrr, hii, modes, imodes, tabs_v[672:704, :96], tabs_v[0:384, :])
+            e0_v[g] = e0
+            s0, s1 = intensity_terms(e0, e1, LOCAL)
+            inten = s0 if inten is None else inten + s0
+            change = s1 if change is None else change + s1
+
+        grids = table_dot(tabs_v[736:800, :96], jnp.concatenate([0.5 * inten, change], 1))
+        hi, lo = split(jnp.concatenate([grids[:, :128], grids[:, 128:]], 0))
+        rows3 = jnp.concatenate([hi, lo, hi], 1)
+        span = 256
+        total = jnp.zeros((4 * SLAB, 256), F32)
+        for c in range(WIDTH // span):
+            part = slice(c * span, (c + 1) * span)
+            full = dot(rows3, up_v[:, part])
+            w0, w1 = weighting(full[:SLAB], full[SLAB:], target_v[:, part])
+            hi, lo = split(jnp.concatenate([w0, w1], 0))
+            total += dot(jnp.concatenate([hi, lo], 0), down_v[part, :])
+        n = 2 * SLAB
+        cols = total[:n, :128] + total[:n, 128:] + total[n:, :128]
+        wgrid = table_dot(tabs_v[800:832, :192], jnp.concatenate([cols[:SLAB], cols[SLAB:]], 1))
+        w0, w1 = wgrid[:, :128], wgrid[:, 128:]
+
+        first = second = None
+        for g in range(KERN):
+            hrr, hii = forms(g)
+            a, b = adjoint_group(
+                e0_v[g], w0, w1, LOCAL, hrr, hii, tabs_v[384:640, :], tabs_v[704:736, :96]
+            )
+            first = a if first is None else first + a
+            second = b if second is None else second + b
+        spectrum = first - times_i(second, sign)
+        y_own[...] = spectrum
+
+        y_copies = exchange(y_own, y_got, y_send, y_recv)
+        arrived(y_copies)
+        whole = combine(spectrum, y_got[1], y_got[0], cr, ci, sign)
+        outs = project(whole, row_tab, col_hi, col_lo, sign)
+        for j in range(2):
+            res_v[j : j + 1, :] = jnp.where(active, outs[j] * (1.0 / math.sqrt(FRAG_LEN)), 0.0)
+
+        res_copies = [
             pltpu.make_async_remote_copy(
-                src_ref=own,
-                dst_ref=got.at[d],
-                send_sem=send.at[d],
-                recv_sem=recv.at[d],
+                src_ref=res_v,
+                dst_ref=res_v,
+                send_sem=res_send.at[d],
+                recv_sem=res_recv.at[0],
                 device_id=device,
                 device_id_type=MESH,
             )
-            for d, (_, device) in enumerate(sides)
+            for d, device in enumerate(others)
         ]
-        for d, (exists, _) in enumerate(sides):
-
-            @pl.when(exists)
-            def _():
-                copies[d].start()
-
-        for d, (exists, _) in enumerate(sides):
-
-            @pl.when(exists)
-            def _():
-                copies[1 - d].wait_recv()
-
-        return copies
-
-    def sent(copies):
-        for d, (exists, _) in enumerate(sides):
-
-            @pl.when(exists)
-            def _():
-                copies[d].wait_send()
-
-    m_copies = exchange(m_own, m_got, m_send, m_recv)
-    modes = combine(modes_own, m_got[1], m_got[0], cr, ci, sign)
-    imodes = times_i(modes, sign)
-
-    for copy in h_copies:
-        copy.wait()
-
-    low = lax.broadcasted_iota(jnp.int32, (ROW_FREQS, 128), 1) < 64
-
-    def forms(g):
-        pairs = [two_forms(h_v[g * LOCAL + k], low) for k in range(LOCAL)]
-        return [a for a, _ in pairs], [b for _, b in pairs]
-
-    inten = change = None
-    for g in range(KERN):
-        hrr, hii = forms(g)
-        e0, e1 = forward_group(hrr, hii, modes, imodes, tabs_v[672:704, :96], tabs_v[0:384, :])
-        e0_v[g] = e0
-        s0, s1 = intensity_terms(e0, e1, LOCAL)
-        inten = s0 if inten is None else inten + s0
-        change = s1 if change is None else change + s1
-
-    grids = table_dot(tabs_v[736:800, :96], jnp.concatenate([0.5 * inten, change], 1))
-    hi, lo = split(jnp.concatenate([grids[:, :128], grids[:, 128:]], 0))
-    rows3 = jnp.concatenate([hi, lo, hi], 1)
-    for copy in later:
-        copy.wait()
-    span = 256
-    total = jnp.zeros((4 * SLAB, 256), F32)
-    for c in range(WIDTH // span):
-        part = slice(c * span, (c + 1) * span)
-        full = dot(rows3, up_v[:, part])
-        w0, w1 = weighting(full[:SLAB], full[SLAB:], target_v[:, part])
-        hi, lo = split(jnp.concatenate([w0, w1], 0))
-        total += dot(jnp.concatenate([hi, lo], 0), down_v[part, :])
-    n = 2 * SLAB
-    cols = total[:n, :128] + total[:n, 128:] + total[n:, :128]
-    wgrid = table_dot(tabs_v[800:832, :192], jnp.concatenate([cols[:SLAB], cols[SLAB:]], 1))
-    w0, w1 = wgrid[:, :128], wgrid[:, 128:]
-
-    first = second = None
-    for g in range(KERN):
-        hrr, hii = forms(g)
-        a, b = adjoint_group(
-            e0_v[g], w0, w1, LOCAL, hrr, hii, tabs_v[384:640, :], tabs_v[704:736, :96]
-        )
-        first = a if first is None else first + a
-        second = b if second is None else second + b
-    spectrum = first - times_i(second, sign)
-    y_own[...] = spectrum
-
-    y_copies = exchange(y_own, y_got, y_send, y_recv)
-    whole = combine(spectrum, y_got[1], y_got[0], cr, ci, sign)
-    outs = project(whole, row_tab, col_hi, col_lo, sign)
-    for j in range(2):
-        out_ref[j : j + 1, :] = jnp.where(active, outs[j] * (1.0 / math.sqrt(FRAG_LEN)), 0.0)
-    sent(m_copies)
-    sent(y_copies)
+        for copy in res_copies:
+            copy.start()
+        sent(m_copies)
+        sent(y_copies)
+        for copy in res_copies:
+            copy.wait_send()
+
+    out_ref[...] = res_v[...]
 
 
 def shards(mask, target, spectra, weights, counts, frag_rows, frag_cols, step):
@@ -490,7 +548,7 @@
     dma = pltpu.SemaphoreType.DMA
     outs = pl.pallas_call(
         kernel,
-        out_shape=jax.ShapeDtypeStruct((2, SLOTS), F32),
+        out_shape=pltpu.VMEM((2, SLOTS), F32),
         in_specs=[hbm] * 13,
         out_specs=vmem,
         scratch_shapes=[
@@ -513,16 +571,21 @@
             pltpu.VMEM((2, 32, 128), F32),
             pltpu.VMEM((32, 128), F32),
             pltpu.VMEM((2, 32, 128), F32),
+            pltpu.VMEM((KERNELS, ROW_FREQS, 128), F32),
+            pltpu.VMEM((KERNELS, ROW_FREQS, 128), F32),
+            pltpu.VMEM((2, SLOTS), F32),
             dma((2 * CHUNKS + 11,)),
-            dma((3,)),
+            dma((1,)),
             dma((3,)),
             dma((2,)),
             dma((2,)),
             dma((2,)),
             dma((2,)),
+            dma((3,)),
+            dma((1,)),
         ],
         compiler_params=pltpu.CompilerParams(
-            collective_id=0, has_side_effects=True, vmem_limit_bytes=64 * 1024 * 1024
+            collective_id=0, has_side_effects=True, vmem_limit_bytes=60 * 1024 * 1024
         ),
     )(
         weights,

time: 27.2 us -> 22.4 us (0.82); the launches traced: 27.1 us -> 22 us
  Pallas kernels: 24.5 us -> 20.1 us
  local copies, waits for them, and re-layouts: 1.32 us -> 0.57 us
    pallas_call x1, Pallas kernels: 24.5 us -> 20.1 us  [shards(): pl.pallas_call(kernel, out_shape=pltpu.VMEM((2, SLOTS), F32), in_specs=[h...]
    slice x1, local copies, waits for them, and re-layouts: 1.32 us -> 0.57 us  [shards(): return (outs[0], outs[1])]
where the time goes in v2:
time: 22.4 us; the launch traced here: 22 us
  Pallas kernels  20.1 us (90%)
  between operations  1.29 us (6%)
  local copies, waits for them, and re-layouts  0.57 us (3%)
    pallas_call x1, Pallas kernels, shards(): pl.pallas_call(kernel, out_shape=pltpu.VMEM((2, SLOTS), F32), in_specs=[h...  20.1 us
    slice x1, local copies, waits for them, and re-layouts, shards(): return (outs[0], outs[1])  0.57 us

profile of v2, /device:TPU:6, one launch (start us, length us, event | category | flops | bytes accessed | tf_op | source)
XLA Modules:
  0.0 22.0 jit_solution(14707884955782178711)
XLA Ops:
  1.3 20.1 %shard_map.140 = f32[2,256]{1,0:T(2,128)S(1)} custom-call(f32[6]{0:T(128)} %weights_hbm.1, s32[1]{0:T(128)S(6)} %copy.15.counts_hbm, s32[1,256]{1,0:T(1,128)} %bitcast.7, s32[1,256]{1,0:T(1,128)} %bitcast.8, f32[1,256]{1,0:T(1,128)} %bitcast.9, f32[6,16,128]{2,1,0:T(8,128)} %spectra_hbm.1, bf16[832,256]{1,0:T(8,128)(2,1)} %constant.10.clone.tabs_hbm, ...), custom_call_target="tpu_custom_call" | custom-call | tf_op jit(solution)/shard_map/pallas_call | solution.py:549
  21.4 0.6 %fusion = (f32[1,256]{1,0:T(1,128)}, f32[1,256]{1,0:T(1,128)}) fusion(f32[2,256]{1,0:T(2,128)S(1)} %shard_map.140), kind=kLoop, calls=%fused_computation | loop fusion | bytes 4096 | tf_op jit(solution)/shard_map/slice | solution.py:605

commit v3 on v2

--- a/solution.py
+++ b/solution.py
@@ -28,6 +28,8 @@
 F32 = jnp.float32
 BF16 = jnp.bfloat16
 CHUNKS = 4
+GROUP = 12
+PLANE = 16
 MESH = pl.DeviceIdType.MESH
 
 
@@ -77,7 +79,8 @@
 
     m = np.arange(GRID_ROWS)
     ang = 2 * np.pi * (np.outer(m, kr) % GRID_ROWS) / GRID_ROWS
-    ag = np.concatenate([np.cos(ang), np.sin(ang)], 1) / math.sqrt(EXT)
+    c, s = np.cos(ang) / math.sqrt(EXT), np.sin(ang) / math.sqrt(EXT)
+    ag = np.block([[c, -s], [s, c]])
     hi, lo = np_split(ag)
     ag3 = np.concatenate([hi, hi, lo], 1)
     hi, lo = np_split(ag.T)
@@ -184,30 +187,29 @@
     return jnp.where(low, h, turned), jnp.where(low, turned, h)
 
 
-def forward_group(hrr, hii, modes, imodes, ag3, inv3):
+def side_by_side(x, rows):
+    return jnp.concatenate([x[i : i + rows] for i in range(0, x.shape[0], rows)], 1)
+
+
+def forward_group(hrr, hii, modes, imodes, inv3, ag3):
     blocks = []
     for j in range(2):
         m, im = modes[16 * j : 16 * j + 16], imodes[16 * j : 16 * j + 16]
-        for k in range(len(hrr)):
-            p = hrr[k] * m + hii[k] * im
-            ip = hrr[k] * im - hii[k] * m
-            blocks.append(jnp.concatenate([p, ip], 0))
-    rows = table_dot(ag3, jnp.concatenate(blocks, 1))
-    stacked = jnp.concatenate([rows[:, 128 * b : 128 * b + 128] for b in range(len(blocks))], 0)
-    hi, lo = split(stacked)
-    amps = dot(jnp.concatenate([hi, lo, hi], 1), inv3)
-    half = amps.shape[0] // 2
-    return amps[:half], amps[half:]
-
-
-def intensity_terms(e0, e1, kernels):
+        blocks += [a * m + b * im for a, b in zip(hrr, hii)]
+    hi, lo = split(jnp.concatenate(blocks, 0))
+    q = dot(jnp.concatenate([hi, lo, hi], 1), inv3)
+    q_re, q_im = side_by_side(q[:, :128], 16), side_by_side(q[:, 128:], 16)
+    return table_dot(ag3, jnp.concatenate([q_re, q_im], 0))
+
+
+def intensity_terms(amps, kernels):
     total0 = total1 = None
     for k in range(kernels):
-        a, b = e0[32 * k : 32 * k + 32], e1[32 * k : 32 * k + 32]
+        a, b = amps[:, 128 * k : 128 * k + 128], amps[:, 128 * (kernels + k) : 128 * (kernels + k) + 128]
         s0, s1 = a * a, a * b
         total0 = s0 if total0 is None else total0 + s0
         total1 = s1 if total1 is None else total1 + s1
-    return total0[:, :128] + total0[:, 128:], total1[:, :128] + total1[:, 128:]
+    return total0[:32] + total0[32:], total1[:32] + total1[32:]
 
 
 def weighting(inten, change, target):
@@ -216,25 +218,26 @@
     return steep * (developed - target), steep * steep * change
 
 
-def adjoint_group(e0, w0, w1, kernels, hrr, hii, adj, agt3):
+def adjoint_group(e0, w0, w1, hrr, hii, adj, agt3):
+    kernels = len(hrr)
     loads = []
     for w in (w0, w1):
-        ww = jnp.concatenate([w, w], 1)
-        for k in range(kernels):
-            loads.append(ww * e0[32 * k : 32 * k + 32])
-    hi, lo = split(jnp.concatenate(loads, 0))
+        ww = jnp.concatenate([w, w], 0)
+        loads += [ww * e0[:, 128 * k : 128 * k + 128] for k in range(kernels)]
+    u = table_dot(agt3, jnp.concatenate(loads, 1))
+    rows = [
+        jnp.concatenate([u[:16, 128 * b : 128 * b + 128], u[16:, 128 * b : 128 * b + 128]], 1)
+        for b in range(2 * kernels)
+    ]
+    hi, lo = split(jnp.concatenate(rows, 0))
     both = dot(hi, adj)
     back = both[:, :128] + both[:, 128:] + dot(lo, adj[:, :128])
-    wide = jnp.concatenate([back[32 * b : 32 * b + 32] for b in range(2 * kernels)], 1)
-    u = table_dot(agt3, wide)
     first, second = [], []
     for j in range(2):
         f = s = None
         for k in range(kernels):
-            at = 128 * (j * kernels + k)
-            u1, u2 = u[:16, at : at + 128], u[16:, at : at + 128]
-            a = hrr[k] * u1 - hii[k] * u2
-            b = hrr[k] * u2 + hii[k] * u1
+            at = 16 * (j * kernels + k)
+            a, b = hrr[k] * back[at : at + 16], hii[k] * back[at : at + 16]
             f = a if f is None else f + a
             s = b if s is None else s + b
         first.append(f)
@@ -306,6 +309,15 @@
         (tile > 0, {"tile": lax.max(tile - 1, 0), "kern": 4 - lead}),
         (tile < TILES - 1, {"tile": lax.min(tile + 1, TILES - 1), "kern": 4 - lead}),
     )
+    first = 1 - lax.min(lax.rem(tile, PLANE), 1)
+    left_of_modes = {
+        "tile": lax.max(tile - 1 - (PLANE - 2) * first, 0),
+        "kern": (4 - lead) * (1 - first),
+    }
+    is_last = jnp.logical_and(lax.rem(tile, PLANE) == PLANE - 1, tile < TILES - 1)
+    is_depot = jnp.logical_and(
+        kern == 0, jnp.logical_and(lax.rem(tile, PLANE) == 1, tile < TILES - PLANE)
+    )
     barrier = pltpu.get_barrier_semaphore()
     used = []
 
@@ -327,11 +339,35 @@
     @pl.when(jnp.logical_not(is_lead))
     def _():
         lead_device = {"tile": tile, "kern": lead}
-        pl.semaphore_signal(barrier, inc=1, device_id=lead_device, device_id_type=MESH)
+
+        @pl.when(is_depot)
+        def _():
+            pl.semaphore_signal(
+                barrier,
+                inc=1,
+                device_id={"tile": lax.min(tile + PLANE - 1, TILES - 1), "kern": 3},
+                device_id_type=MESH,
+            )
+
         for copy in early:
             copy.start()
         scale_own()
-        pl.semaphore_wait(barrier, 1)
+        pl.semaphore_wait(barrier, 1 + is_depot.astype(jnp.int32))
+
+        @pl.when(is_depot)
+        def _():
+            copy = pltpu.make_async_remote_copy(
+                src_ref=m_got.at[0],
+                dst_ref=m_got.at[0],
+                send_sem=m_send.at[0],
+                recv_sem=m_recv.at[0],
+                device_id={"tile": lax.min(tile + PLANE - 2, TILES - 1), "kern": 1},
+                device_id_type=MESH,
+            )
+            copy.wait_recv()
+            copy.start()
+            copy.wait_send()
+
         place = lax.rem(kern - lead + KERN, KERN) - 1
         copy = pltpu.make_async_remote_copy(
             src_ref=h_v.at[pl.ds(mine, LOCAL)],
@@ -361,7 +397,16 @@
                 m_got[1 - d] = jnp.zeros((32, 128), F32)
                 y_got[1 - d] = jnp.zeros((32, 128), F32)
 
-        for exists, device in sides:
+        @pl.when(is_last)
+        def _():
+            pl.semaphore_signal(
+                barrier,
+                inc=1,
+                device_id={"tile": lax.max(tile - (PLANE - 2), 0), "kern": 0},
+                device_id_type=MESH,
+            )
+
+        for exists, device in (sides[0], (jnp.logical_and(sides[1][0], jnp.logical_not(is_last)), sides[1][1])):
 
             @pl.when(exists)
             def _():
@@ -412,7 +457,7 @@
         modes_own = own_modes(packed, row_tab, col_hi, col_lo, amp, tabs_v[640:672, :192], sign)
         m_own[...] = modes_own
 
-        def exchange(own, got, send, recv):
+        def exchange(own, got, send, recv, devices):
             copies = [
                 pltpu.make_async_remote_copy(
                     src_ref=own,
@@ -422,7 +467,7 @@
                     device_id=device,
                     device_id_type=MESH,
                 )
-                for d, (_, device) in enumerate(sides)
+                for d, device in enumerate(devices)
             ]
             for d, (exists, _) in enumerate(sides):
 
@@ -446,8 +491,8 @@
                 def _():
                     copies[d].wait_send()
 
-        pl.semaphore_wait(barrier, 3 + lax.min(tile, 1) + lax.min(TILES - 1 - tile, 1))
-        m_copies = exchange(m_own, m_got, m_send, m_recv)
+        pl.semaphore_wait(barrier, lax.min(tile, 1) + lax.min(TILES - 1 - tile, 1))
+        m_copies = exchange(m_own, m_got, m_send, m_recv, (left_of_modes, sides[1][1]))
 
         scale_own()
         low = lax.broadcasted_iota(jnp.int32, (ROW_FREQS, 128), 1) < 64
@@ -468,7 +513,7 @@
                 hii_v[d * LOCAL + k] = b
 
         def forms(g):
-            ks = range(g * LOCAL, (g + 1) * LOCAL)
+            ks = range(g * GROUP, (g + 1) * GROUP)
             return [hrr_v[k] for k in ks], [hii_v[k] for k in ks]
 
         for copy in later:
@@ -478,15 +523,15 @@
         imodes = times_i(modes, sign)
 
         inten = change = None
-        for g in range(KERN):
+        for g in range(KERNELS // GROUP):
             hrr, hii = forms(g)
-            e0, e1 = forward_group(hrr, hii, modes, imodes, tabs_v[672:704, :96], tabs_v[0:384, :])
-            e0_v[g] = e0
-            s0, s1 = intensity_terms(e0, e1, LOCAL)
+            amps = forward_group(hrr, hii, modes, imodes, tabs_v[0:384, :], tabs_v[672:736, :96])
+            e0_v[g] = amps[:, : 128 * GROUP]
+            s0, s1 = intensity_terms(amps, GROUP)
             inten = s0 if inten is None else inten + s0
             change = s1 if change is None else change + s1
 
-        grids = table_dot(tabs_v[736:800, :96], jnp.concatenate([0.5 * inten, change], 1))
+        grids = table_dot(tabs_v[768:832, :96], jnp.concatenate([0.5 * inten, change], 1))
         hi, lo = split(jnp.concatenate([grids[:, :128], grids[:, 128:]], 0))
         rows3 = jnp.concatenate([hi, lo, hi], 1)
         span = 256
@@ -499,21 +544,21 @@
             total += dot(jnp.concatenate([hi, lo], 0), down_v[part, :])
         n = 2 * SLAB
         cols = total[:n, :128] + total[:n, 128:] + total[n:, :128]
-        wgrid = table_dot(tabs_v[800:832, :192], jnp.concatenate([cols[:SLAB], cols[SLAB:]], 1))
+        wgrid = table_dot(tabs_v[832:864, :192], jnp.concatenate([cols[:SLAB], cols[SLAB:]], 1))
         w0, w1 = wgrid[:, :128], wgrid[:, 128:]
 
         first = second = None
-        for g in range(KERN):
+        for g in range(KERNELS // GROUP):
             hrr, hii = forms(g)
             a, b = adjoint_group(
-                e0_v[g], w0, w1, LOCAL, hrr, hii, tabs_v[384:640, :], tabs_v[704:736, :96]
+                e0_v[g], w0, w1, hrr, hii, tabs_v[384:640, :], tabs_v[736:768, :192]
             )
             first = a if first is None else first + a
             second = b if second is None else second + b
         spectrum = first - times_i(second, sign)
         y_own[...] = spectrum
 
-        y_copies = exchange(y_own, y_got, y_send, y_recv)
+        y_copies = exchange(y_own, y_got, y_send, y_recv, (sides[0][1], sides[1][1]))
         arrived(y_copies)
         whole = combine(spectrum, y_got[1], y_got[0], cr, ci, sign)
         outs = project(whole, row_tab, col_hi, col_lo, sign)
@@ -531,8 +576,8 @@
             )
             for d, device in enumerate(others)
         ]
-        for copy in res_copies:
-            copy.start()
+        for d in (1, 0, 2):
+            res_copies[d].start()
         sent(m_copies)
         sent(y_copies)
         for copy in res_copies:
@@ -566,7 +611,7 @@
             pltpu.VMEM((384, WIDTH), BF16),
             pltpu.VMEM((WIDTH, 256), BF16),
             pltpu.VMEM((KERNELS, ROW_FREQS, 128), F32),
-            pltpu.VMEM((KERN, LOCAL * GRID_ROWS, 256), F32),
+            pltpu.VMEM((KERNELS // GROUP, 2 * GRID_ROWS, 128 * GROUP), F32),
             pltpu.VMEM((32, 128), F32),
             pltpu.VMEM((2, 32, 128), F32),
             pltpu.VMEM((32, 128), F32),

time: 22.4 us -> 20.6 us (0.920); the launches traced: 22 us -> 20.5 us
  Pallas kernels: 20.1 us -> 18.6 us
    pallas_call x1, Pallas kernels: 20.1 us -> 18.6 us  [shards(): pl.pallas_call(kernel, out_shape=pltpu.VMEM((2, SLOTS), F32), in_specs=[h...]
where the time goes in v3:
time: 20.6 us; the launch traced here: 20.5 us
  Pallas kernels  18.6 us (90%)
  between operations  1.29 us (6%)
  local copies, waits for them, and re-layouts  0.57 us (3%)
    pallas_call x1, Pallas kernels, shards(): pl.pallas_call(kernel, out_shape=pltpu.VMEM((2, SLOTS), F32), in_specs=[h...  18.6 us
    slice x1, local copies, waits for them, and re-layouts, shards(): return (outs[0], outs[1])  0.57 us

profile of v3, /device:TPU:6, one launch (start us, length us, event | category | flops | bytes accessed | tf_op | source)
XLA Modules:
  0.0 20.5 jit_solution(4833690699585533727)
XLA Ops:
  1.3 18.6 %shard_map.140 = f32[2,256]{1,0:T(2,128)S(1)} custom-call(f32[6]{0:T(128)} %weights_hbm.1, s32[1]{0:T(128)S(6)} %copy.15.counts_hbm, s32[1,256]{1,0:T(1,128)} %bitcast.7, s32[1,256]{1,0:T(1,128)} %bitcast.8, f32[1,256]{1,0:T(1,128)} %bitcast.9, f32[6,16,128]{2,1,0:T(8,128)} %spectra_hbm.1, bf16[864,256]{1,0:T(8,128)(2,1)} %constant.10.clone.tabs_hbm, ...), custom_call_target="tpu_custom_call" | custom-call | tf_op jit(solution)/shard_map/pallas_call | solution.py:594
  19.9 0.6 %fusion = (f32[1,256]{1,0:T(1,128)}, f32[1,256]{1,0:T(1,128)}) fusion(f32[2,256]{1,0:T(2,128)S(1)} %shard_map.140), kind=kLoop, calls=%fused_computation | loop fusion | bytes 4096 | tf_op jit(solution)/shard_map/slice | solution.py:650

commit v4 on v3

--- a/solution.py
+++ b/solution.py
@@ -27,8 +27,12 @@
 THRESH = 0.1
 F32 = jnp.float32
 BF16 = jnp.bfloat16
-CHUNKS = 4
-GROUP = 12
+CHUNKS = 2
+GROUP = 6
+SPAN = 256
+AHEAD = 1
+AGROUP = 6
+AAHEAD = 1
 PLANE = 16
 MESH = pl.DeviceIdType.MESH
 
@@ -59,10 +63,10 @@
     for kap in range(1, COL_FREQS):
         base += 2 * np.cos(2 * np.pi * ((np.arange(WIDTH) * kap) % WIDTH) / WIDTH)
     g = (base / GRID_COLS)[dist]
+    g = g[:, : WIDTH // 2]
     g_hi, g_lo = np_split(g)
-    up = np.concatenate([g_hi, g_hi, g_lo], 0)
-    gt_hi, gt_lo = np_split(g.T)
-    down = np.concatenate([gt_hi, gt_lo], 1)
+    up = np.concatenate([g_hi.T, g_hi.T, g_lo.T], 1)
+    down = np.concatenate([g_hi, g_lo], 0)
 
     ang = 2 * np.pi * (np.outer(kc, n) % GRID_COLS) / GRID_COLS
     c, s = np.cos(ang) / math.sqrt(WIDTH), np.sin(ang) / math.sqrt(WIDTH)
@@ -84,7 +88,7 @@
     hi, lo = np_split(ag)
     ag3 = np.concatenate([hi, hi, lo], 1)
     hi, lo = np_split(ag.T)
-    agt3 = np.concatenate([hi, hi, lo], 1)
+    agt3 = np.concatenate([np.concatenate([hi, hi], 1), np.concatenate([lo, lo], 1)], 0)
 
     rstep = EXT // GRID_ROWS
     dist = (e[:, None] - rstep * m[None, :]) % EXT
@@ -94,11 +98,11 @@
     r = (base / GRID_ROWS)[dist]
     hi, lo = np_split(r)
     r3 = np.concatenate([hi, hi, lo], 1)
-    hi, lo = np_split(r.T)
-    rt3 = np.concatenate([hi, hi, lo], 1)
+    hi, lo = np_split(np.concatenate([r.T, r.T], 1))
+    rt2 = np.concatenate([hi, lo], 1)
 
     tabs = np.concatenate(
-        [inv3, adj, pad_lanes(lt3), pad_lanes(ag3), pad_lanes(agt3), pad_lanes(r3), pad_lanes(rt3)], 0
+        [inv3, adj, pad_lanes(lt3), pad_lanes(ag3), pad_lanes(agt3), pad_lanes(r3), rt2], 0
     )
 
     ang = 2 * np.pi * (kr % 3) / 3
@@ -128,6 +132,32 @@
 def table_dot(table3, x):
     hi, lo = split(x)
     return dot(table3, jnp.concatenate([hi, lo, hi], 0))
+
+
+def with_halves_swapped(x):
+    return pltpu.roll(x, 64, axis=1)
+
+
+def column_rows(grids):
+    i, d = grids[:, :128], grids[:, 128:]
+    hi, lo = split(jnp.concatenate([i, with_halves_swapped(i), d, with_halves_swapped(d)], 0))
+    return jnp.concatenate([hi, lo, hi], 1)
+
+
+def weighted_back(full, target, down):
+    w0, w1 = weighting(full[:, :128], full[:, 128:], target)
+    hi, lo = split(jnp.concatenate([w0, w1], 1))
+    both = dot(down, hi)
+    return both[:128] + both[128:] + dot(down[:128], lo)
+
+
+def weighted_grid(z, rt2):
+    swapped = jnp.concatenate([z[64:], z[:64]], 0)
+    low = (lax.broadcasted_iota(jnp.int32, z.shape, 1) & 64) == 0
+    v = jnp.where(low, z, swapped)
+    hi, lo = split(jnp.concatenate([v[:, :128], v[:, 128:]], 0))
+    rt_hi, rt_lo = rt2[:, :128], rt2[:, 128:]
+    return dot_nt(jnp.concatenate([rt_hi, rt_hi, rt_lo], 1), jnp.concatenate([hi, lo, hi], 1))
 
 
 def sin_turns(u):
@@ -191,13 +221,16 @@
     return jnp.concatenate([x[i : i + rows] for i in range(0, x.shape[0], rows)], 1)
 
 
-def forward_group(hrr, hii, modes, imodes, inv3, ag3):
+def forward_group(hrr, hii, modes, imodes, inv3):
     blocks = []
     for j in range(2):
         m, im = modes[16 * j : 16 * j + 16], imodes[16 * j : 16 * j + 16]
-        blocks += [a * m + b * im for a, b in zip(hrr, hii)]
+        blocks += [hrr[k] * m + hii[k] * im for k in range(hrr.shape[0])]
     hi, lo = split(jnp.concatenate(blocks, 0))
-    q = dot(jnp.concatenate([hi, lo, hi], 1), inv3)
+    return dot(jnp.concatenate([hi, lo, hi], 1), inv3)
+
+
+def forward_rows(q, ag3):
     q_re, q_im = side_by_side(q[:, :128], 16), side_by_side(q[:, 128:], 16)
     return table_dot(ag3, jnp.concatenate([q_re, q_im], 0))
 
@@ -218,13 +251,19 @@
     return steep * (developed - target), steep * steep * change
 
 
-def adjoint_group(e0, w0, w1, hrr, hii, adj, agt3):
-    kernels = len(hrr)
+def adjoint_rows(e0, w0, w1, agt3):
+    kernels = e0.shape[1] // 128
     loads = []
     for w in (w0, w1):
         ww = jnp.concatenate([w, w], 0)
         loads += [ww * e0[:, 128 * k : 128 * k + 128] for k in range(kernels)]
-    u = table_dot(agt3, jnp.concatenate(loads, 1))
+    hi, lo = split(jnp.concatenate(loads, 1))
+    u = dot(agt3, jnp.concatenate([hi, lo], 0))
+    return u[:32] + u[32:]
+
+
+def adjoint_columns(u, hrr, hii, adj):
+    kernels = hrr.shape[0]
     rows = [
         jnp.concatenate([u[:16, 128 * b : 128 * b + 128], u[16:, 128 * b : 128 * b + 128]], 1)
         for b in range(2 * kernels)
@@ -289,6 +328,7 @@
     y_got,
     hrr_v,
     hii_v,
+    turned_v,
     res_v,
     load_sem,
     h_send,
@@ -431,10 +471,12 @@
         mask_copies = [load(mask_hbm.at[:, p], mask_v.at[:, p]) for p in parts]
         fwd_copies = [load(fwd_hbm.at[p, :], fwd_v.at[p, :]) for p in parts]
         later = [load(up_hbm, up_v), load(target_hbm, target_v), load(down_hbm, down_v)]
+        for copy in small:
+            copy.start()
         for a, b in zip(mask_copies, fwd_copies):
             a.start()
             b.start()
-        for copy in early + small + later:
+        for copy in early + later:
             copy.start()
 
         for copy in small:
@@ -496,7 +538,8 @@
 
         scale_own()
         low = lax.broadcasted_iota(jnp.int32, (ROW_FREQS, 128), 1) < 64
-        for d in range(KERN):
+
+        def take(place, d):
             at = pl.multiple_of(lax.rem(lead + d, KERN) * LOCAL, LOCAL)
             if d > 0:
                 pltpu.make_async_remote_copy(
@@ -509,52 +552,67 @@
                 ).wait_recv()
             for k in range(LOCAL):
                 a, b = two_forms(h_v[at + k], low)
-                hrr_v[d * LOCAL + k] = a
-                hii_v[d * LOCAL + k] = b
+                hrr_v[place * LOCAL + k] = a
+                hii_v[place * LOCAL + k] = b
+
+        take(0, 0)
+        take(1, 3)
 
         def forms(g):
-            ks = range(g * GROUP, (g + 1) * GROUP)
-            return [hrr_v[k] for k in ks], [hii_v[k] for k in ks]
+            ks = pl.ds(g * GROUP, GROUP)
+            return hrr_v[ks], hii_v[ks]
 
         for copy in later:
             copy.wait()
+        for c in range(8):
+            ends = [target_v[:, h + 128 * c : h + 128 * c + 128] for h in (0, WIDTH // 2)]
+            turned_v[128 * c : 128 * c + 128, :] = jnp.transpose(jnp.concatenate(ends, 0))
         arrived(m_copies)
         modes = combine(modes_own, m_got[1], m_got[0], cr, ci, sign)
         imodes = times_i(modes, sign)
 
-        inten = change = None
-        for g in range(KERNELS // GROUP):
-            hrr, hii = forms(g)
-            amps = forward_group(hrr, hii, modes, imodes, tabs_v[0:384, :], tabs_v[672:736, :96])
-            e0_v[g] = amps[:, : 128 * GROUP]
-            s0, s1 = intensity_terms(amps, GROUP)
-            inten = s0 if inten is None else inten + s0
-            change = s1 if change is None else change + s1
-
-        grids = table_dot(tabs_v[768:832, :96], jnp.concatenate([0.5 * inten, change], 1))
-        hi, lo = split(jnp.concatenate([grids[:, :128], grids[:, 128:]], 0))
-        rows3 = jnp.concatenate([hi, lo, hi], 1)
-        span = 256
-        total = jnp.zeros((4 * SLAB, 256), F32)
-        for c in range(WIDTH // span):
-            part = slice(c * span, (c + 1) * span)
-            full = dot(rows3, up_v[:, part])
-            w0, w1 = weighting(full[:SLAB], full[SLAB:], target_v[:, part])
-            hi, lo = split(jnp.concatenate([w0, w1], 0))
-            total += dot(jnp.concatenate([hi, lo], 0), down_v[part, :])
-        n = 2 * SLAB
-        cols = total[:n, :128] + total[:n, 128:] + total[n:, :128]
-        wgrid = table_dot(tabs_v[832:864, :192], jnp.concatenate([cols[:SLAB], cols[SLAB:]], 1))
+        inten = change = jnp.zeros((GRID_ROWS, 128), F32)
+        n = KERNELS // GROUP
+        ready = []
+        for g in range(n + AHEAD):
+            if g == n // 2:
+                take(2, 2)
+            if g == max(3 * n // 4, 1):
+                take(3, 1)
+            if g < n:
+                hrr, hii = forms(g)
+                ready.append(forward_group(hrr, hii, modes, imodes, tabs_v[0:384, :]))
+            if g >= AHEAD:
+                amps = forward_rows(ready[g - AHEAD], tabs_v[672:736, :96])
+                e0_v[g - AHEAD] = amps[:, : 128 * GROUP]
+                s0, s1 = intensity_terms(amps, GROUP)
+                inten, change = inten + s0, change + s1
+
+        grids = table_dot(tabs_v[800:864, :96], jnp.concatenate([0.5 * inten, change], 1))
+        rows3 = column_rows(grids)
+
+        n = WIDTH // 2 // SPAN
+        parts = [slice(c * SPAN, (c + 1) * SPAN) for c in range(n)]
+        total = jnp.zeros((128, 256), F32)
+        full = dot_nt(up_v[parts[0], :], rows3)
+        for c in range(n):
+            ahead = dot_nt(up_v[parts[c + 1], :], rows3) if c + 1 < n else None
+            total += weighted_back(full, turned_v[parts[c], :], down_v[:, parts[c]])
+            full = ahead
+        wgrid = weighted_grid(total, tabs_v[864:896, :])
         w0, w1 = wgrid[:, :128], wgrid[:, 128:]
 
-        first = second = None
-        for g in range(KERNELS // GROUP):
-            hrr, hii = forms(g)
-            a, b = adjoint_group(
-                e0_v[g], w0, w1, hrr, hii, tabs_v[384:640, :], tabs_v[736:768, :192]
-            )
-            first = a if first is None else first + a
-            second = b if second is None else second + b
+        first = second = jnp.zeros((32, 128), F32)
+        ready = []
+        n = KERNELS // AGROUP
+        for g in range(n + AAHEAD):
+            if g < n:
+                e0 = e0_v[g * AGROUP // GROUP, :, pl.ds(g * AGROUP % GROUP * 128, AGROUP * 128)]
+                ready.append(adjoint_rows(e0, w0, w1, tabs_v[736:800, :128]))
+            if g >= AAHEAD:
+                ks = pl.ds((g - AAHEAD) * AGROUP, AGROUP)
+                a, b = adjoint_columns(ready[g - AAHEAD], hrr_v[ks], hii_v[ks], tabs_v[384:640, :])
+                first, second = first + a, second + b
         spectrum = first - times_i(second, sign)
         y_own[...] = spectrum
 
@@ -608,8 +666,8 @@
             pltpu.VMEM((SLAB, WIDTH), F32),
             pltpu.VMEM((SLAB, WIDTH), F32),
             pltpu.VMEM((WIDTH, 256), BF16),
-            pltpu.VMEM((384, WIDTH), BF16),
-            pltpu.VMEM((WIDTH, 256), BF16),
+            pltpu.VMEM(up.shape, BF16),
+            pltpu.VMEM(down.shape, BF16),
             pltpu.VMEM((KERNELS, ROW_FREQS, 128), F32),
             pltpu.VMEM((KERNELS // GROUP, 2 * GRID_ROWS, 128 * GROUP), F32),
             pltpu.VMEM((32, 128), F32),
@@ -618,6 +676,7 @@
             pltpu.VMEM((2, 32, 128), F32),
             pltpu.VMEM((KERNELS, ROW_FREQS, 128), F32),
             pltpu.VMEM((KERNELS, ROW_FREQS, 128), F32),
+            pltpu.VMEM((WIDTH // 2, 128), F32),
             pltpu.VMEM((2, SLOTS), F32),
             dma((2 * CHUNKS + 11,)),
             dma((1,)),

time: 20.6 us -> 20.8 us (level)
  no operation moved by 1% of the time
where the time goes in v4:
time: 20.8 us; the launch traced here: 20.7 us
  Pallas kernels  18.8 us (90%)
  between operations  1.29 us (6%)
  local copies, waits for them, and re-layouts  0.57 us (3%)
    pallas_call x1, Pallas kernels, shards(): pl.pallas_call(kernel, out_shape=pltpu.VMEM((2, SLOTS), F32), in_specs=[h...  18.8 us
    slice x1, local copies, waits for them, and re-layouts, shards(): return (outs[0], outs[1])  0.57 us

profile of v4, /device:TPU:6, one launch (start us, length us, event | category | flops | bytes accessed | tf_op | source)
XLA Modules:
  0.0 20.7 jit_solution(10422072995058089927)
XLA Ops:
  1.3 18.8 %shard_map.140 = f32[2,256]{1,0:T(2,128)S(1)} custom-call(f32[6]{0:T(128)} %weights_hbm.1, s32[1]{0:T(128)S(6)} %copy.15.counts_hbm, s32[1,256]{1,0:T(1,128)} %bitcast.5, s32[1,256]{1,0:T(1,128)} %bitcast.6, f32[1,256]{1,0:T(1,128)} %bitcast.7, f32[6,16,128]{2,1,0:T(8,128)} %spectra_hbm.1, bf16[896,256]{1,0:T(8,128)(2,1)} %constant.10.clone.tabs_hbm, ...), custom_call_target="tpu_custom_call" | custom-call | tf_op jit(solution)/shard_map/pallas_call | solution.py:652
  20.1 0.6 %fusion = (f32[1,256]{1,0:T(1,128)}, f32[1,256]{1,0:T(1,128)}) fusion(f32[2,256]{1,0:T(2,128)S(1)} %shard_map.140), kind=kLoop, calls=%fused_computation | loop fusion | bytes 4096 | tf_op jit(solution)/shard_map/slice | solution.py:709

commit v5 on v4

--- a/solution.py
+++ b/solution.py
@@ -28,10 +28,10 @@
 F32 = jnp.float32
 BF16 = jnp.bfloat16
 CHUNKS = 2
-GROUP = 6
+GROUP = 8
 SPAN = 256
 AHEAD = 1
-AGROUP = 6
+AGROUP = 8
 AAHEAD = 1
 PLANE = 16
 MESH = pl.DeviceIdType.MESH
@@ -339,25 +339,32 @@
     y_recv,
     res_send,
     res_recv,
+    go_sem,
 ):
     tile = lax.axis_index("tile")
     kern = lax.axis_index("kern")
-    lead = 3 - 2 * lax.rem(tile, 2)
+    def depot_tile(t):
+        return jnp.logical_and(lax.rem(t, PLANE) == 1, t < TILES - PLANE).astype(jnp.int32)
+
+    def lead_of(t):
+        return 3 - 2 * lax.rem(t, 2) - depot_tile(t)
+
+    lead = lead_of(tile)
     is_lead = kern == lead
     others = [{"tile": tile, "kern": lax.rem(lead + d, KERN)} for d in (1, 2, 3)]
+    before, after = lax.max(tile - 1, 0), lax.min(tile + 1, TILES - 1)
     sides = (
-        (tile > 0, {"tile": lax.max(tile - 1, 0), "kern": 4 - lead}),
-        (tile < TILES - 1, {"tile": lax.min(tile + 1, TILES - 1), "kern": 4 - lead}),
+        (tile > 0, {"tile": before, "kern": lead_of(before)}),
+        (tile < TILES - 1, {"tile": after, "kern": lead_of(after)}),
     )
     first = 1 - lax.min(lax.rem(tile, PLANE), 1)
     left_of_modes = {
         "tile": lax.max(tile - 1 - (PLANE - 2) * first, 0),
-        "kern": (4 - lead) * (1 - first),
+        "kern": lead_of(before) * (1 - first) + first,
     }
     is_last = jnp.logical_and(lax.rem(tile, PLANE) == PLANE - 1, tile < TILES - 1)
-    is_depot = jnp.logical_and(
-        kern == 0, jnp.logical_and(lax.rem(tile, PLANE) == 1, tile < TILES - PLANE)
-    )
+    has_depot = depot_tile(tile) == 1
+    is_depot = jnp.logical_and(has_depot, kern == 1)
     barrier = pltpu.get_barrier_semaphore()
     used = []
 
@@ -388,25 +395,19 @@
                 device_id={"tile": lax.min(tile + PLANE - 1, TILES - 1), "kern": 3},
                 device_id_type=MESH,
             )
+            pl.semaphore_signal(barrier, inc=1, device_id=lead_device, device_id_type=MESH)
 
         for copy in early:
             copy.start()
         scale_own()
-        pl.semaphore_wait(barrier, 1 + is_depot.astype(jnp.int32))
 
         @pl.when(is_depot)
         def _():
-            copy = pltpu.make_async_remote_copy(
-                src_ref=m_got.at[0],
-                dst_ref=m_got.at[0],
-                send_sem=m_send.at[0],
-                recv_sem=m_recv.at[0],
-                device_id={"tile": lax.min(tile + PLANE - 2, TILES - 1), "kern": 1},
-                device_id_type=MESH,
-            )
-            copy.wait_recv()
-            copy.start()
-            copy.wait_send()
+            pl.semaphore_wait(go_sem, 1)
+
+        @pl.when(jnp.logical_not(is_depot))
+        def _():
+            pl.semaphore_wait(barrier, 1)
 
         place = lax.rem(kern - lead + KERN, KERN) - 1
         copy = pltpu.make_async_remote_copy(
@@ -418,6 +419,22 @@
             device_id_type=MESH,
         )
         copy.start()
+
+        @pl.when(is_depot)
+        def _():
+            pl.semaphore_wait(barrier, 1)
+            onward = pltpu.make_async_remote_copy(
+                src_ref=m_got.at[0],
+                dst_ref=m_got.at[0],
+                send_sem=m_send.at[0],
+                recv_sem=m_recv.at[0],
+                device_id={"tile": lax.min(tile + PLANE - 2, TILES - 1), "kern": 1},
+                device_id_type=MESH,
+            )
+            onward.wait_recv()
+            onward.start()
+            onward.wait_send()
+
         copy.wait_send()
         pltpu.make_async_remote_copy(
             src_ref=res_v,
@@ -442,7 +459,7 @@
             pl.semaphore_signal(
                 barrier,
                 inc=1,
-                device_id={"tile": lax.max(tile - (PLANE - 2), 0), "kern": 0},
+                device_id={"tile": lax.max(tile - (PLANE - 2), 0), "kern": 1},
                 device_id_type=MESH,
             )
 
@@ -452,8 +469,12 @@
             def _():
                 pl.semaphore_signal(barrier, inc=1, device_id=device, device_id_type=MESH)
 
-        for device in others:
+        for device in others[1:]:
             pl.semaphore_signal(barrier, inc=1, device_id=device, device_id_type=MESH)
+
+        @pl.when(jnp.logical_not(has_depot))
+        def _():
+            pl.semaphore_signal(barrier, inc=1, device_id=others[0], device_id_type=MESH)
 
         width = WIDTH // CHUNKS
         small = [
@@ -533,7 +554,14 @@
                 def _():
                     copies[d].wait_send()
 
-        pl.semaphore_wait(barrier, lax.min(tile, 1) + lax.min(TILES - 1 - tile, 1))
+        pl.semaphore_wait(
+            barrier, lax.min(tile, 1) + lax.min(TILES - 1 - tile, 1) + depot_tile(tile)
+        )
+
+        @pl.when(has_depot)
+        def _():
+            pl.semaphore_signal(go_sem, inc=1, device_id=others[0], device_id_type=MESH)
+
         m_copies = exchange(m_own, m_got, m_send, m_recv, (left_of_modes, sides[1][1]))
 
         scale_own()
@@ -687,6 +715,7 @@
             dma((2,)),
             dma((3,)),
             dma((1,)),
+            pltpu.SemaphoreType.REGULAR,
         ],
         compiler_params=pltpu.CompilerParams(
             collective_id=0, has_side_effects=True, vmem_limit_bytes=60 * 1024 * 1024

time: 20.8 us -> 20.1 us (0.966)
  Pallas kernels: 18.8 us -> 18.1 us
    pallas_call x1, Pallas kernels: 18.8 us -> 18.1 us  [shards(): pl.pallas_call(kernel, out_shape=pltpu.VMEM((2, SLOTS), F32), in_specs=[h...]
where the time goes in v5:
time: 20.1 us; the launch traced here: 20 us
  Pallas kernels  18.1 us (90%)
  between operations  1.29 us (6%)
  local copies, waits for them, and re-layouts  0.57 us (3%)
    pallas_call x1, Pallas kernels, shards(): pl.pallas_call(kernel, out_shape=pltpu.VMEM((2, SLOTS), F32), in_specs=[h...  18.1 us
    slice x1, local copies, waits for them, and re-layouts, shards(): return (outs[0], outs[1])  0.57 us

profile of v5, /device:TPU:6, one launch (start us, length us, event | category | flops | bytes accessed | tf_op | source)
XLA Modules:
  0.0 20.0 jit_solution(3109687926444535318)
XLA Ops:
  1.3 18.1 %shard_map.140 = f32[2,256]{1,0:T(2,128)S(1)} custom-call(f32[6]{0:T(128)} %weights_hbm.1, s32[1]{0:T(128)S(6)} %copy.15.counts_hbm, s32[1,256]{1,0:T(1,128)} %bitcast.5, s32[1,256]{1,0:T(1,128)} %bitcast.6, f32[1,256]{1,0:T(1,128)} %bitcast.7, f32[6,16,128]{2,1,0:T(8,128)} %spectra_hbm.1, bf16[896,256]{1,0:T(8,128)(2,1)} %constant.10.clone.tabs_hbm, ...), custom_call_target="tpu_custom_call" | custom-call | tf_op jit(solution)/shard_map/pallas_call | solution.py:680
  19.4 0.6 %fusion = (f32[1,256]{1,0:T(1,128)}, f32[1,256]{1,0:T(1,128)}) fusion(f32[2,256]{1,0:T(2,128)S(1)} %shard_map.140), kind=kLoop, calls=%fused_computation | loop fusion | bytes 4096 | tf_op jit(solution)/shard_map/slice | solution.py:738

commit v6 on v5

--- a/solution.py
+++ b/solution.py
@@ -340,6 +340,8 @@
     res_send,
     res_recv,
     go_sem,
+    own_recv,
+    far_sem,
 ):
     tile = lax.axis_index("tile")
     kern = lax.axis_index("kern")
@@ -363,7 +365,15 @@
         "kern": lead_of(before) * (1 - first) + first,
     }
     is_last = jnp.logical_and(lax.rem(tile, PLANE) == PLANE - 1, tile < TILES - 1)
+    is_first = jnp.logical_and(first == 1, tile > 0)
     has_depot = depot_tile(tile) == 1
+
+    def far_of(t):
+        base = 2 - 2 * (lead_of(t) // 2)
+        return [{"tile": t, "kern": base + c} for c in range(2)]
+
+    is_far = kern // 2 != lead // 2
+    mate = {"tile": tile, "kern": lead + 1 - 2 * lax.rem(lead, 2)}
     is_depot = jnp.logical_and(has_depot, kern == 1)
     barrier = pltpu.get_barrier_semaphore()
     used = []
@@ -383,9 +393,42 @@
             scale = jnp.sqrt(jnp.full((ROW_FREQS, 128), weights_s[k] * (2.0 / KERNELS), F32))
             h_v[mine + k] = spectra_v[k] * scale
 
+    def fragments():
+        sign = lane_sign((32, 128))
+        cr, ci = consts_v[0:32], consts_v[32:64]
+        dsc = consts_v[64:192]
+        row_tab, col_tab = fragment_tables(rows_v[...], cols_v[...], jnp.concatenate([dsc, dsc], 1))
+        col_hi, col_lo = split(col_tab)
+        active = lax.broadcasted_iota(jnp.int32, (1, SLOTS), 1) < counts_s[0]
+        return sign, cr, ci, row_tab, col_hi, col_lo, active
+
+    def finish(spectrum, sign, cr, ci, row_tab, col_hi, col_lo, active):
+        whole = combine(spectrum, y_got[1], y_got[0], cr, ci, sign)
+        outs = project(whole, row_tab, col_hi, col_lo, sign)
+        for j in range(2):
+            res_v[j : j + 1, :] = jnp.where(active, outs[j] * (1.0 / math.sqrt(FRAG_LEN)), 0.0)
+
     @pl.when(jnp.logical_not(is_lead))
     def _():
         lead_device = {"tile": tile, "kern": lead}
+        small = [
+            load(a, b)
+            for a, b in (
+                (counts_hbm, counts_s),
+                (rows_hbm, rows_v),
+                (cols_hbm, cols_v),
+                (consts_hbm, consts_v),
+            )
+        ]
+
+        @pl.when(is_far)
+        def _():
+            for d, (exists, _) in enumerate(sides):
+
+                @pl.when(jnp.logical_not(exists))
+                def _():
+                    y_got[1 - d] = jnp.zeros((32, 128), F32)
+
 
         @pl.when(is_depot)
         def _():
@@ -433,17 +476,57 @@
             )
             onward.wait_recv()
             onward.start()
+            pl.semaphore_wait(far_sem.at[0], 1)
+            pl.semaphore_signal(
+                far_sem.at[0],
+                inc=1,
+                device_id={"tile": lax.min(tile + PLANE - 2, TILES - 1), "kern": 1},
+                device_id_type=MESH,
+            )
             onward.wait_send()
 
+        @pl.when(jnp.logical_not(is_far))
+        def _():
+            pltpu.make_async_remote_copy(
+                src_ref=res_v,
+                dst_ref=res_v,
+                send_sem=res_send.at[0],
+                recv_sem=res_recv.at[0],
+                device_id=lead_device,
+                device_id_type=MESH,
+            ).wait_recv()
+
+        @pl.when(is_far)
+        def _():
+            for load_copy in small:
+                load_copy.start()
+            for load_copy in small:
+                load_copy.wait()
+            sign, cr, ci, row_tab, col_hi, col_lo, active = fragments()
+            for d, (exists, _) in enumerate(sides):
+
+                @pl.when(exists)
+                def _():
+                    pltpu.make_async_remote_copy(
+                        src_ref=y_own,
+                        dst_ref=y_got.at[1 - d],
+                        send_sem=y_send.at[0],
+                        recv_sem=y_recv.at[1 - d],
+                        device_id=lead_device,
+                        device_id_type=MESH,
+                    ).wait_recv()
+
+            pltpu.make_async_remote_copy(
+                src_ref=y_own,
+                dst_ref=y_own,
+                send_sem=y_send.at[0],
+                recv_sem=own_recv.at[0],
+                device_id=lead_device,
+                device_id_type=MESH,
+            ).wait_recv()
+            finish(y_own[...], sign, cr, ci, row_tab, col_hi, col_lo, active)
+
         copy.wait_send()
-        pltpu.make_async_remote_copy(
-            src_ref=res_v,
-            dst_ref=res_v,
-            send_sem=res_send.at[0],
-            recv_sem=res_recv.at[0],
-            device_id=lead_device,
-            device_id_type=MESH,
-        ).wait_recv()
 
     @pl.when(is_lead)
     def _():
@@ -463,18 +546,18 @@
                 device_id_type=MESH,
             )
 
+        @pl.when(jnp.logical_not(has_depot))
+        def _():
+            pl.semaphore_signal(barrier, inc=1, device_id=others[0], device_id_type=MESH)
+
+        for device in others[1:]:
+            pl.semaphore_signal(barrier, inc=1, device_id=device, device_id_type=MESH)
+
         for exists, device in (sides[0], (jnp.logical_and(sides[1][0], jnp.logical_not(is_last)), sides[1][1])):
 
             @pl.when(exists)
             def _():
                 pl.semaphore_signal(barrier, inc=1, device_id=device, device_id_type=MESH)
-
-        for device in others[1:]:
-            pl.semaphore_signal(barrier, inc=1, device_id=device, device_id_type=MESH)
-
-        @pl.when(jnp.logical_not(has_depot))
-        def _():
-            pl.semaphore_signal(barrier, inc=1, device_id=others[0], device_id_type=MESH)
 
         width = WIDTH // CHUNKS
         small = [
@@ -502,12 +585,7 @@
 
         for copy in small:
             copy.wait()
-        sign = lane_sign((32, 128))
-        cr, ci = consts_v[0:32], consts_v[32:64]
-        dsc = consts_v[64:192]
-        row_tab, col_tab = fragment_tables(rows_v[...], cols_v[...], jnp.concatenate([dsc, dsc], 1))
-        col_hi, col_lo = split(col_tab)
-        active = lax.broadcasted_iota(jnp.int32, (1, SLOTS), 1) < counts_s[0]
+        sign, cr, ci, row_tab, col_hi, col_lo, active = fragments()
         amp = jnp.where(active, step_v[...], 0.0) * (1.0 / math.sqrt(FRAG_LEN))
 
         total = jnp.zeros((2 * SLAB, 256), F32)
@@ -567,17 +645,39 @@
         scale_own()
         low = lax.broadcasted_iota(jnp.int32, (ROW_FREQS, 128), 1) < 64
 
+        def spectra_from(d):
+            at = pl.multiple_of(lax.rem(lead + d, KERN) * LOCAL, LOCAL)
+            return pltpu.make_async_remote_copy(
+                src_ref=h_v.at[pl.ds(at, LOCAL)],
+                dst_ref=h_v.at[pl.ds(at, LOCAL)],
+                send_sem=h_send.at[0],
+                recv_sem=h_recv.at[d - 1],
+                device_id=others[0],
+                device_id_type=MESH,
+            )
+
+        def far_is_here(d):
+            pl.semaphore_signal(
+                far_sem.at[d],
+                inc=1,
+                device_id=(left_of_modes, sides[1][1])[d],
+                device_id_type=MESH,
+            )
+
+        @pl.when(is_first)
+        def _():
+            for d in (1, 2, 3):
+                spectra_from(d).wait_recv()
+            far_is_here(0)
+
         def take(place, d):
             at = pl.multiple_of(lax.rem(lead + d, KERN) * LOCAL, LOCAL)
             if d > 0:
-                pltpu.make_async_remote_copy(
-                    src_ref=h_v.at[pl.ds(at, LOCAL)],
-                    dst_ref=h_v.at[pl.ds(at, LOCAL)],
-                    send_sem=h_send.at[0],
-                    recv_sem=h_recv.at[d - 1],
-                    device_id=others[0],
-                    device_id_type=MESH,
-                ).wait_recv()
+
+                @pl.when(jnp.logical_not(is_first))
+                def _():
+                    spectra_from(d).wait_recv()
+
             for k in range(LOCAL):
                 a, b = two_forms(h_v[at + k], low)
                 hrr_v[place * LOCAL + k] = a
@@ -607,6 +707,15 @@
                 take(2, 2)
             if g == max(3 * n // 4, 1):
                 take(3, 1)
+
+                @pl.when(jnp.logical_and(sides[0][0], jnp.logical_not(is_first)))
+                def _():
+                    far_is_here(0)
+
+                @pl.when(sides[1][0])
+                def _():
+                    far_is_here(1)
+
             if g < n:
                 hrr, hii = forms(g)
                 ready.append(forward_group(hrr, hii, modes, imodes, tabs_v[0:384, :]))
@@ -644,30 +753,58 @@
         spectrum = first - times_i(second, sign)
         y_own[...] = spectrum
 
-        y_copies = exchange(y_own, y_got, y_send, y_recv, (sides[0][1], sides[1][1]))
-        arrived(y_copies)
-        whole = combine(spectrum, y_got[1], y_got[0], cr, ci, sign)
-        outs = project(whole, row_tab, col_hi, col_lo, sign)
-        for j in range(2):
-            res_v[j : j + 1, :] = jnp.where(active, outs[j] * (1.0 / math.sqrt(FRAG_LEN)), 0.0)
-
-        res_copies = [
-            pltpu.make_async_remote_copy(
-                src_ref=res_v,
-                dst_ref=res_v,
-                send_sem=res_send.at[d],
-                recv_sem=res_recv.at[0],
+        def send_own(i, device, d=None):
+            return pltpu.make_async_remote_copy(
+                src_ref=y_own,
+                dst_ref=y_own if d is None else y_got.at[d],
+                send_sem=y_send.at[i],
+                recv_sem=own_recv.at[0] if d is None else y_recv.at[d],
                 device_id=device,
                 device_id_type=MESH,
             )
-            for d, device in enumerate(others)
+
+        y_copies = [send_own(d, sides[d][1], d) for d in range(2)]
+        own_copies = [send_own(2 + c, device) for c, device in enumerate(far_of(tile))]
+        far_copies = [
+            [send_own(4 + 2 * d + c, device, d) for c, device in enumerate(far_of(t))]
+            for d, t in enumerate((before, after))
         ]
-        for d in (1, 0, 2):
-            res_copies[d].start()
+        for d in (1, 0):
+
+            @pl.when(sides[d][0])
+            def _():
+                pl.semaphore_wait(far_sem.at[1 - d], 1)
+                for copy in reversed(far_copies[d]):
+                    copy.start()
+                y_copies[d].start()
+
+            if d == 1:
+                for copy in own_copies:
+                    copy.start()
+
+        arrived(y_copies)
+        finish(spectrum, sign, cr, ci, row_tab, col_hi, col_lo, active)
+        res_copy = pltpu.make_async_remote_copy(
+            src_ref=res_v,
+            dst_ref=res_v,
+            send_sem=res_send.at[0],
+            recv_sem=res_recv.at[0],
+            device_id=mate,
+            device_id_type=MESH,
+        )
+        res_copy.start()
         sent(m_copies)
         sent(y_copies)
-        for copy in res_copies:
+        for copy in own_copies:
             copy.wait_send()
+        for d in range(2):
+
+            @pl.when(sides[d][0])
+            def _():
+                for copy in far_copies[d]:
+                    copy.wait_send()
+
+        res_copy.wait_send()
 
     out_ref[...] = res_v[...]
 
@@ -706,16 +843,18 @@
             pltpu.VMEM((KERNELS, ROW_FREQS, 128), F32),
             pltpu.VMEM((WIDTH // 2, 128), F32),
             pltpu.VMEM((2, SLOTS), F32),
-            dma((2 * CHUNKS + 11,)),
+            dma((2 * CHUNKS + 15,)),
             dma((1,)),
             dma((3,)),
             dma((2,)),
             dma((2,)),
+            dma((8,)),
             dma((2,)),
-            dma((2,)),
-            dma((3,)),
+            dma((1,)),
             dma((1,)),
             pltpu.SemaphoreType.REGULAR,
+            dma((1,)),
+            pltpu.SemaphoreType.REGULAR((2,)),
         ],
         compiler_params=pltpu.CompilerParams(
             collective_id=0, has_side_effects=True, vmem_limit_bytes=60 * 1024 * 1024

time: 20.1 us -> 19.8 us (0.985)
  Pallas kernels: 18.1 us -> 17.8 us
    pallas_call x1, Pallas kernels: 18.1 us -> 17.8 us  [shards(): pl.pallas_call(kernel, out_shape=pltpu.VMEM((2, SLOTS), F32), in_specs=[h...]
where the time goes in v6:
time: 19.8 us; the launch traced here: 19.6 us
  Pallas kernels  17.8 us (90%)
  between operations  1.29 us (7%)
  local copies, waits for them, and re-layouts  0.57 us (3%)
    pallas_call x1, Pallas kernels, shards(): pl.pallas_call(kernel, out_shape=pltpu.VMEM((2, SLOTS), F32), in_specs=[h...  17.8 us
    slice x1, local copies, waits for them, and re-layouts, shards(): return (outs[0], outs[1])  0.57 us

profile of v6, /device:TPU:6, one launch (start us, length us, event | category | flops | bytes accessed | tf_op | source)
XLA Modules:
  0.0 19.6 jit_solution(6726885982579325436)
XLA Ops:
  1.3 17.8 %shard_map.140 = f32[2,256]{1,0:T(2,128)S(1)} custom-call(f32[6]{0:T(128)} %weights_hbm.1, s32[1]{0:T(128)S(6)} %copy.15.counts_hbm, s32[1,256]{1,0:T(1,128)} %bitcast.5, s32[1,256]{1,0:T(1,128)} %bitcast.6, f32[1,256]{1,0:T(1,128)} %bitcast.7, f32[6,16,128]{2,1,0:T(8,128)} %spectra_hbm.1, bf16[896,256]{1,0:T(8,128)(2,1)} %constant.10.clone.tabs_hbm, ...), custom_call_target="tpu_custom_call" | custom-call | tf_op jit(solution)/shard_map/pallas_call | solution.py:817
  19.0 0.6 %fusion = (f32[1,256]{1,0:T(1,128)}, f32[1,256]{1,0:T(1,128)}) fusion(f32[2,256]{1,0:T(2,128)S(1)} %shard_map.140), kind=kLoop, calls=%fused_computation | loop fusion | bytes 4096 | tf_op jit(solution)/shard_map/slice | solution.py:877

commit v7 on v6

--- a/solution.py
+++ b/solution.py
@@ -345,6 +345,18 @@
 ):
     tile = lax.axis_index("tile")
     kern = lax.axis_index("kern")
+    barrier = pltpu.get_barrier_semaphore()
+    is_last = jnp.logical_and(lax.rem(tile, PLANE) == PLANE - 1, tile < TILES - 1)
+
+    @pl.when(jnp.logical_and(is_last, kern == 1))
+    def _():
+        pl.semaphore_signal(
+            barrier,
+            inc=1,
+            device_id={"tile": lax.max(tile - (PLANE - 2), 0), "kern": 1},
+            device_id_type=MESH,
+        )
+
     def depot_tile(t):
         return jnp.logical_and(lax.rem(t, PLANE) == 1, t < TILES - PLANE).astype(jnp.int32)
 
@@ -364,7 +376,6 @@
         "tile": lax.max(tile - 1 - (PLANE - 2) * first, 0),
         "kern": lead_of(before) * (1 - first) + first,
     }
-    is_last = jnp.logical_and(lax.rem(tile, PLANE) == PLANE - 1, tile < TILES - 1)
     is_first = jnp.logical_and(first == 1, tile > 0)
     has_depot = depot_tile(tile) == 1
 
@@ -375,7 +386,6 @@
     is_far = kern // 2 != lead // 2
     mate = {"tile": tile, "kern": lead + 1 - 2 * lax.rem(lead, 2)}
     is_depot = jnp.logical_and(has_depot, kern == 1)
-    barrier = pltpu.get_barrier_semaphore()
     used = []
 
     def load(src, dst):
@@ -536,15 +546,6 @@
             def _():
                 m_got[1 - d] = jnp.zeros((32, 128), F32)
                 y_got[1 - d] = jnp.zeros((32, 128), F32)
-
-        @pl.when(is_last)
-        def _():
-            pl.semaphore_signal(
-                barrier,
-                inc=1,
-                device_id={"tile": lax.max(tile - (PLANE - 2), 0), "kern": 1},
-                device_id_type=MESH,
-            )
 
         @pl.when(jnp.logical_not(has_depot))
         def _():
@@ -695,6 +696,7 @@
         for c in range(8):
             ends = [target_v[:, h + 128 * c : h + 128 * c + 128] for h in (0, WIDTH // 2)]
             turned_v[128 * c : 128 * c + 128, :] = jnp.transpose(jnp.concatenate(ends, 0))
+        take(2, 2)
         arrived(m_copies)
         modes = combine(modes_own, m_got[1], m_got[0], cr, ci, sign)
         imodes = times_i(modes, sign)
@@ -703,8 +705,6 @@
         n = KERNELS // GROUP
         ready = []
         for g in range(n + AHEAD):
-            if g == n // 2:
-                take(2, 2)
             if g == max(3 * n // 4, 1):
                 take(3, 1)
 

time: 19.8 us -> 19.6 us (0.990)
  Pallas kernels: 17.8 us -> 17.6 us
where the time goes in v7:
time: 19.6 us; the launch traced here: 19.5 us
  Pallas kernels  17.6 us (90%)
  between operations  1.29 us (7%)
  local copies, waits for them, and re-layouts  0.57 us (3%)
    pallas_call x1, Pallas kernels, shards(): pl.pallas_call(kernel, out_shape=pltpu.VMEM((2, SLOTS), F32), in_specs=[h...  17.6 us
    slice x1, local copies, waits for them, and re-layouts, shards(): return (outs[0], outs[1])  0.57 us

profile of v7, /device:TPU:6, one launch (start us, length us, event | category | flops | bytes accessed | tf_op | source)
XLA Modules:
  0.0 19.5 jit_solution(3333798926094172268)
XLA Ops:
  1.3 17.6 %shard_map.140 = f32[2,256]{1,0:T(2,128)S(1)} custom-call(f32[6]{0:T(128)} %weights_hbm.1, s32[1]{0:T(128)S(6)} %copy.15.counts_hbm, s32[1,256]{1,0:T(1,128)} %bitcast.5, s32[1,256]{1,0:T(1,128)} %bitcast.6, f32[1,256]{1,0:T(1,128)} %bitcast.7, f32[6,16,128]{2,1,0:T(8,128)} %spectra_hbm.1, bf16[896,256]{1,0:T(8,128)(2,1)} %constant.10.clone.tabs_hbm, ...), custom_call_target="tpu_custom_call" | custom-call | tf_op jit(solution)/shard_map/pallas_call | solution.py:817
  18.9 0.6 %fusion = (f32[1,256]{1,0:T(1,128)}, f32[1,256]{1,0:T(1,128)}) fusion(f32[2,256]{1,0:T(2,128)S(1)} %shard_map.140), kind=kLoop, calls=%fused_computation | loop fusion | bytes 4096 | tf_op jit(solution)/shard_map/slice | solution.py:877

commit v8 on v7

--- a/solution.py
+++ b/solution.py
@@ -27,7 +27,7 @@
 THRESH = 0.1
 F32 = jnp.float32
 BF16 = jnp.bfloat16
-CHUNKS = 2
+CHUNKS = 1
 GROUP = 8
 SPAN = 256
 AHEAD = 1
@@ -209,7 +209,11 @@
 
 
 def combine(own, left, right, cr, ci, sign):
-    return own + cr * (left + right) + ci * times_i(left - right, sign)
+    both, odd = left + right, left - right
+    return (
+        own + cr * both + ci * times_i(odd, sign),
+        times_i(own, sign) + cr * times_i(both, sign) - ci * odd,
+    )
 
 
 def two_forms(h, low):
@@ -284,8 +288,7 @@
     return jnp.concatenate(first, 0), jnp.concatenate(second, 0)
 
 
-def project(total, row_tab, col_hi, col_lo, sign):
-    it = times_i(total, sign)
+def project(total, it, row_tab, col_hi, col_lo):
     lhs = jnp.concatenate([total[:16], it[:16], total[16:], it[16:]], 0)
     hi, lo = split(lhs)
     q = dot(jnp.concatenate([hi, lo, hi], 1), jnp.concatenate([col_hi, col_hi, col_lo], 0))
@@ -294,7 +297,7 @@
 
 def kernel(
     weights_hbm,
-    counts_hbm,
+    counts_s,
     rows_hbm,
     cols_hbm,
     step_hbm,
@@ -308,7 +311,6 @@
     down_hbm,
     out_ref,
     weights_s,
-    counts_s,
     rows_v,
     cols_v,
     step_v,
@@ -331,16 +333,9 @@
     turned_v,
     res_v,
     load_sem,
-    h_send,
     h_recv,
-    m_send,
     m_recv,
-    y_send,
     y_recv,
-    res_send,
-    res_recv,
-    go_sem,
-    own_recv,
     far_sem,
 ):
     tile = lax.axis_index("tile")
@@ -414,7 +409,7 @@
 
     def finish(spectrum, sign, cr, ci, row_tab, col_hi, col_lo, active):
         whole = combine(spectrum, y_got[1], y_got[0], cr, ci, sign)
-        outs = project(whole, row_tab, col_hi, col_lo, sign)
+        outs = project(*whole, row_tab, col_hi, col_lo)
         for j in range(2):
             res_v[j : j + 1, :] = jnp.where(active, outs[j] * (1.0 / math.sqrt(FRAG_LEN)), 0.0)
 
@@ -424,7 +419,6 @@
         small = [
             load(a, b)
             for a, b in (
-                (counts_hbm, counts_s),
                 (rows_hbm, rows_v),
                 (cols_hbm, cols_v),
                 (consts_hbm, consts_v),
@@ -456,7 +450,7 @@
 
         @pl.when(is_depot)
         def _():
-            pl.semaphore_wait(go_sem, 1)
+            pl.semaphore_wait(far_sem.at[1], 1)
 
         @pl.when(jnp.logical_not(is_depot))
         def _():
@@ -466,7 +460,7 @@
         copy = pltpu.make_async_remote_copy(
             src_ref=h_v.at[pl.ds(mine, LOCAL)],
             dst_ref=h_v.at[pl.ds(mine, LOCAL)],
-            send_sem=h_send.at[0],
+            send_sem=load_sem.at[5],
             recv_sem=h_recv.at[place],
             device_id=lead_device,
             device_id_type=MESH,
@@ -479,7 +473,7 @@
             onward = pltpu.make_async_remote_copy(
                 src_ref=m_got.at[0],
                 dst_ref=m_got.at[0],
-                send_sem=m_send.at[0],
+                send_sem=load_sem.at[6],
                 recv_sem=m_recv.at[0],
                 device_id={"tile": lax.min(tile + PLANE - 2, TILES - 1), "kern": 1},
                 device_id_type=MESH,
@@ -500,8 +494,8 @@
             pltpu.make_async_remote_copy(
                 src_ref=res_v,
                 dst_ref=res_v,
-                send_sem=res_send.at[0],
-                recv_sem=res_recv.at[0],
+                send_sem=load_sem.at[0],
+                recv_sem=h_recv.at[0],
                 device_id=lead_device,
                 device_id_type=MESH,
             ).wait_recv()
@@ -520,7 +514,7 @@
                     pltpu.make_async_remote_copy(
                         src_ref=y_own,
                         dst_ref=y_got.at[1 - d],
-                        send_sem=y_send.at[0],
+                        send_sem=load_sem.at[0],
                         recv_sem=y_recv.at[1 - d],
                         device_id=lead_device,
                         device_id_type=MESH,
@@ -529,8 +523,8 @@
             pltpu.make_async_remote_copy(
                 src_ref=y_own,
                 dst_ref=y_own,
-                send_sem=y_send.at[0],
-                recv_sem=own_recv.at[0],
+                send_sem=load_sem.at[0],
+                recv_sem=h_recv.at[1],
                 device_id=lead_device,
                 device_id_type=MESH,
             ).wait_recv()
@@ -560,11 +554,11 @@
             def _():
                 pl.semaphore_signal(barrier, inc=1, device_id=device, device_id_type=MESH)
 
+        del used[2:]
         width = WIDTH // CHUNKS
         small = [
             load(a, b)
             for a, b in (
-                (counts_hbm, counts_s),
                 (rows_hbm, rows_v),
                 (cols_hbm, cols_v),
                 (step_hbm, step_v),
@@ -599,12 +593,12 @@
         modes_own = own_modes(packed, row_tab, col_hi, col_lo, amp, tabs_v[640:672, :192], sign)
         m_own[...] = modes_own
 
-        def exchange(own, got, send, recv, devices):
+        def exchange(own, got, recv, devices):
             copies = [
                 pltpu.make_async_remote_copy(
                     src_ref=own,
                     dst_ref=got.at[d],
-                    send_sem=send.at[d],
+                    send_sem=load_sem.at[2 + d],
                     recv_sem=recv.at[d],
                     device_id=device,
                     device_id_type=MESH,
@@ -639,9 +633,9 @@
 
         @pl.when(has_depot)
         def _():
-            pl.semaphore_signal(go_sem, inc=1, device_id=others[0], device_id_type=MESH)
-
-        m_copies = exchange(m_own, m_got, m_send, m_recv, (left_of_modes, sides[1][1]))
+            pl.semaphore_signal(far_sem.at[1], inc=1, device_id=others[0], device_id_type=MESH)
+
+        m_copies = exchange(m_own, m_got, m_recv, (left_of_modes, sides[1][1]))
 
         scale_own()
         low = lax.broadcasted_iota(jnp.int32, (ROW_FREQS, 128), 1) < 64
@@ -651,7 +645,7 @@
             return pltpu.make_async_remote_copy(
                 src_ref=h_v.at[pl.ds(at, LOCAL)],
                 dst_ref=h_v.at[pl.ds(at, LOCAL)],
-                send_sem=h_send.at[0],
+                send_sem=load_sem.at[0],
                 recv_sem=h_recv.at[d - 1],
                 device_id=others[0],
                 device_id_type=MESH,
@@ -698,8 +692,7 @@
             turned_v[128 * c : 128 * c + 128, :] = jnp.transpose(jnp.concatenate(ends, 0))
         take(2, 2)
         arrived(m_copies)
-        modes = combine(modes_own, m_got[1], m_got[0], cr, ci, sign)
-        imodes = times_i(modes, sign)
+        modes, imodes = combine(modes_own, m_got[1], m_got[0], cr, ci, sign)
 
         inten = change = jnp.zeros((GRID_ROWS, 128), F32)
         n = KERNELS // GROUP
@@ -757,8 +750,8 @@
             return pltpu.make_async_remote_copy(
                 src_ref=y_own,
                 dst_ref=y_own if d is None else y_got.at[d],
-                send_sem=y_send.at[i],
-                recv_sem=own_recv.at[0] if d is None else y_recv.at[d],
+                send_sem=load_sem.at[4 + i],
+                recv_sem=h_recv.at[1] if d is None else y_recv.at[d],
                 device_id=device,
                 device_id_type=MESH,
             )
@@ -787,8 +780,8 @@
         res_copy = pltpu.make_async_remote_copy(
             src_ref=res_v,
             dst_ref=res_v,
-            send_sem=res_send.at[0],
-            recv_sem=res_recv.at[0],
+            send_sem=load_sem.at[0],
+            recv_sem=h_recv.at[0],
             device_id=mate,
             device_id_type=MESH,
         )
@@ -817,11 +810,10 @@
     outs = pl.pallas_call(
         kernel,
         out_shape=pltpu.VMEM((2, SLOTS), F32),
-        in_specs=[hbm] * 13,
+        in_specs=[hbm, pl.BlockSpec(memory_space=pltpu.SMEM)] + [hbm] * 11,
         out_specs=vmem,
         scratch_shapes=[
             pltpu.SMEM((LOCAL,), F32),
-            pltpu.SMEM((1,), jnp.int32),
             pltpu.VMEM((1, SLOTS), jnp.int32),
             pltpu.VMEM((1, SLOTS), jnp.int32),
             pltpu.VMEM((1, SLOTS), F32),
@@ -843,17 +835,10 @@
             pltpu.VMEM((KERNELS, ROW_FREQS, 128), F32),
             pltpu.VMEM((WIDTH // 2, 128), F32),
             pltpu.VMEM((2, SLOTS), F32),
-            dma((2 * CHUNKS + 15,)),
-            dma((1,)),
+            dma((2 * CHUNKS + 10,)),
             dma((3,)),
             dma((2,)),
             dma((2,)),
-            dma((8,)),
-            dma((2,)),
-            dma((1,)),
-            dma((1,)),
-            pltpu.SemaphoreType.REGULAR,
-            dma((1,)),
             pltpu.SemaphoreType.REGULAR((2,)),
         ],
         compiler_params=pltpu.CompilerParams(

time: 19.6 us -> 19.3 us (0.985)
  Pallas kernels: 17.6 us -> 17.3 us
    pallas_call x1, Pallas kernels: 17.6 us -> 17.3 us  [shards(): pl.pallas_call(kernel, out_shape=pltpu.VMEM((2, SLOTS), F32), in_specs=[h...]
where the time goes in v8:
time: 19.3 us; the launch traced here: 19.1 us
  Pallas kernels  17.3 us (90%)
  between operations  1.29 us (7%)
  local copies, waits for them, and re-layouts  0.57 us (3%)
    pallas_call x1, Pallas kernels, shards(): pl.pallas_call(kernel, out_shape=pltpu.VMEM((2, SLOTS), F32), in_specs=[h...  17.3 us
    slice x1, local copies, waits for them, and re-layouts, shards(): return (outs[0], outs[1])  0.57 us

profile of v8, /device:TPU:6, one launch (start us, length us, event | category | flops | bytes accessed | tf_op | source)
XLA Modules:
  0.0 19.1 jit_solution(13677129379103045126)
XLA Ops:
  1.3 17.3 %shard_map.140 = f32[2,256]{1,0:T(2,128)S(1)} custom-call(f32[6]{0:T(128)} %weights_hbm.1, s32[1]{0:T(128)S(6)} %copy.15.counts_s, s32[1,256]{1,0:T(1,128)} %bitcast.5, s32[1,256]{1,0:T(1,128)} %bitcast.6, f32[1,256]{1,0:T(1,128)} %bitcast.7, f32[6,16,128]{2,1,0:T(8,128)} %spectra_hbm.1, bf16[896,256]{1,0:T(8,128)(2,1)} %constant.10.clone.tabs_hbm, ...), custom_call_target="tpu_custom_call" | custom-call | tf_op jit(solution)/shard_map/pallas_call | solution.py:810
  18.6 0.6 %fusion = (f32[1,256]{1,0:T(1,128)}, f32[1,256]{1,0:T(1,128)}) fusion(f32[2,256]{1,0:T(2,128)S(1)} %shard_map.140), kind=kLoop, calls=%fused_computation | loop fusion | bytes 4096 | tf_op jit(solution)/shard_map/slice | solution.py:862

commit v9 on v8

--- a/solution.py
+++ b/solution.py
@@ -65,7 +65,7 @@
     g = (base / GRID_COLS)[dist]
     g = g[:, : WIDTH // 2]
     g_hi, g_lo = np_split(g)
-    up = np.concatenate([g_hi.T, g_hi.T, g_lo.T], 1)
+    up = np.concatenate([g_hi.T, g_lo.T], 1)
     down = np.concatenate([g_hi, g_lo], 0)
 
     ang = 2 * np.pi * (np.outer(kc, n) % GRID_COLS) / GRID_COLS
@@ -113,7 +113,9 @@
     d = d / math.sqrt(WIDTH)
     col = np.concatenate([cr, ci, d, -d])
     consts = np.repeat(col[:, None], 128, 1).astype(np.float32)
-    return fwd, up, down, tabs, consts
+    blocks = [down[:, i : i + SPAN] for i in range(0, WIDTH // 2, SPAN)]
+    first = np.concatenate([tabs, fwd], 0)
+    return first, np.concatenate([up] + blocks, 0), consts
 
 
 def split(x):
@@ -306,9 +308,7 @@
     consts_hbm,
     mask_hbm,
     target_hbm,
-    fwd_hbm,
-    up_hbm,
-    down_hbm,
+    later_hbm,
     out_ref,
     weights_s,
     rows_v,
@@ -319,9 +319,7 @@
     consts_v,
     mask_v,
     target_v,
-    fwd_v,
-    up_v,
-    down_v,
+    later_v,
     h_v,
     e0_v,
     m_own,
@@ -335,7 +333,6 @@
     load_sem,
     h_recv,
     m_recv,
-    y_recv,
     far_sem,
 ):
     tile = lax.axis_index("tile")
@@ -515,7 +512,7 @@
                         src_ref=y_own,
                         dst_ref=y_got.at[1 - d],
                         send_sem=load_sem.at[0],
-                        recv_sem=y_recv.at[1 - d],
+                        recv_sem=h_recv.at[2 - 2 * d],
                         device_id=lead_device,
                         device_id_type=MESH,
                     ).wait_recv()
@@ -563,13 +560,12 @@
                 (cols_hbm, cols_v),
                 (step_hbm, step_v),
                 (consts_hbm, consts_v),
-                (tabs_hbm, tabs_v),
             )
         ]
         parts = [pl.ds(c * width, width) for c in range(CHUNKS)]
         mask_copies = [load(mask_hbm.at[:, p], mask_v.at[:, p]) for p in parts]
-        fwd_copies = [load(fwd_hbm.at[p, :], fwd_v.at[p, :]) for p in parts]
-        later = [load(up_hbm, up_v), load(target_hbm, target_v), load(down_hbm, down_v)]
+        fwd_copies = [load(tabs_hbm, tabs_v)]
+        later = [load(later_hbm, later_v), load(target_hbm, target_v)]
         for copy in small:
             copy.start()
         for a, b in zip(mask_copies, fwd_copies):
@@ -588,7 +584,7 @@
             mask_copies[c].wait()
             fwd_copies[c].wait()
             hi, lo = split(mask_v[:, c * width : (c + 1) * width])
-            total += dot(jnp.concatenate([hi, lo], 0), fwd_v[c * width : (c + 1) * width, :])
+            total += dot(jnp.concatenate([hi, lo], 0), tabs_v[896 + c * width : 896 + (c + 1) * width, :])
         packed = total[:SLAB, :128] + total[:SLAB, 128:] + total[SLAB:, :128]
         modes_own = own_modes(packed, row_tab, col_hi, col_lo, amp, tabs_v[640:672, :192], sign)
         m_own[...] = modes_own
@@ -724,10 +720,18 @@
         n = WIDTH // 2 // SPAN
         parts = [slice(c * SPAN, (c + 1) * SPAN) for c in range(n)]
         total = jnp.zeros((128, 256), F32)
-        full = dot_nt(up_v[parts[0], :], rows3)
+
+        def up(c):
+            u = later_v[parts[c], :]
+            return jnp.concatenate([u[:, :128], u[:, :128], u[:, 128:]], 1)
+
+        def down(c):
+            return later_v[WIDTH // 2 + SPAN * c : WIDTH // 2 + SPAN * c + 256, :]
+
+        full = dot_nt(up(0), rows3)
         for c in range(n):
-            ahead = dot_nt(up_v[parts[c + 1], :], rows3) if c + 1 < n else None
-            total += weighted_back(full, turned_v[parts[c], :], down_v[:, parts[c]])
+            ahead = dot_nt(up(c + 1), rows3) if c + 1 < n else None
+            total += weighted_back(full, turned_v[parts[c], :], down(c))
             full = ahead
         wgrid = weighted_grid(total, tabs_v[864:896, :])
         w0, w1 = wgrid[:, :128], wgrid[:, 128:]
@@ -745,13 +749,14 @@
                 first, second = first + a, second + b
         spectrum = first - times_i(second, sign)
         y_own[...] = spectrum
+        sent(m_copies)
 
         def send_own(i, device, d=None):
             return pltpu.make_async_remote_copy(
                 src_ref=y_own,
                 dst_ref=y_own if d is None else y_got.at[d],
-                send_sem=load_sem.at[4 + i],
-                recv_sem=h_recv.at[1] if d is None else y_recv.at[d],
+                send_sem=load_sem.at[2 + i],
+                recv_sem=h_recv.at[1] if d is None else h_recv.at[2 * d],
                 device_id=device,
                 device_id_type=MESH,
             )
@@ -786,7 +791,6 @@
             device_id_type=MESH,
         )
         res_copy.start()
-        sent(m_copies)
         sent(y_copies)
         for copy in own_copies:
             copy.wait_send()
@@ -803,14 +807,14 @@
 
 
 def shards(mask, target, spectra, weights, counts, frag_rows, frag_cols, step):
-    fwd, up, down, tabs, consts = make_tables()
+    tabs, later_tabs, consts = make_tables()
     vmem = pl.BlockSpec(memory_space=pltpu.VMEM)
     hbm = pl.BlockSpec(memory_space=pltpu.HBM)
     dma = pltpu.SemaphoreType.DMA
     outs = pl.pallas_call(
         kernel,
         out_shape=pltpu.VMEM((2, SLOTS), F32),
-        in_specs=[hbm, pl.BlockSpec(memory_space=pltpu.SMEM)] + [hbm] * 11,
+        in_specs=[hbm, pl.BlockSpec(memory_space=pltpu.SMEM)] + [hbm] * 9,
         out_specs=vmem,
         scratch_shapes=[
             pltpu.SMEM((LOCAL,), F32),
@@ -822,9 +826,7 @@
             pltpu.VMEM(consts.shape, F32),
             pltpu.VMEM((SLAB, WIDTH), F32),
             pltpu.VMEM((SLAB, WIDTH), F32),
-            pltpu.VMEM((WIDTH, 256), BF16),
-            pltpu.VMEM(up.shape, BF16),
-            pltpu.VMEM(down.shape, BF16),
+            pltpu.VMEM(later_tabs.shape, BF16),
             pltpu.VMEM((KERNELS, ROW_FREQS, 128), F32),
             pltpu.VMEM((KERNELS // GROUP, 2 * GRID_ROWS, 128 * GROUP), F32),
             pltpu.VMEM((32, 128), F32),
@@ -835,9 +837,8 @@
             pltpu.VMEM((KERNELS, ROW_FREQS, 128), F32),
             pltpu.VMEM((WIDTH // 2, 128), F32),
             pltpu.VMEM((2, SLOTS), F32),
-            dma((2 * CHUNKS + 10,)),
+            dma((10,)),
             dma((3,)),
-            dma((2,)),
             dma((2,)),
             pltpu.SemaphoreType.REGULAR((2,)),
         ],
@@ -855,9 +856,7 @@
         jnp.asarray(consts),
         mask,
         target,
-        jnp.asarray(fwd),
-        jnp.asarray(up),
-        jnp.asarray(down),
+        jnp.asarray(later_tabs),
     )
     return outs[0], outs[1]
 

time: 19.3 us -> 19.3 us (level)
  no operation moved by 1% of the time
where the time goes in v9:
time: 19.3 us; the launch traced here: 19.1 us
  Pallas kernels  17.2 us (89%)
  between operations  1.29 us (7%)
  local copies, waits for them, and re-layouts  0.57 us (3%)
    pallas_call x1, Pallas kernels, shards(): pl.pallas_call(kernel, out_shape=pltpu.VMEM((2, SLOTS), F32), in_specs=[h...  17.2 us
    slice x1, local copies, waits for them, and re-layouts, shards(): return (outs[0], outs[1])  0.57 us

profile of v9, /device:TPU:6, one launch (start us, length us, event | category | flops | bytes accessed | tf_op | source)
XLA Modules:
  0.0 19.1 jit_solution(7136862693234858580)
XLA Ops:
  1.3 17.2 %shard_map.122 = f32[2,256]{1,0:T(2,128)S(1)} custom-call(f32[6]{0:T(128)} %weights_hbm.1, s32[1]{0:T(128)S(6)} %copy.13.counts_s, s32[1,256]{1,0:T(1,128)} %bitcast.7, s32[1,256]{1,0:T(1,128)} %bitcast.8, f32[1,256]{1,0:T(1,128)} %bitcast.9, f32[6,16,128]{2,1,0:T(8,128)} %spectra_hbm.1, bf16[2944,256]{1,0:T(8,128)(2,1)} %constant.6.clone.tabs_hbm, ...), custom_call_target="tpu_custom_call" | custom-call | tf_op jit(solution)/shard_map/pallas_call | solution.py:814
  18.5 0.6 %fusion = (f32[1,256]{1,0:T(1,128)}, f32[1,256]{1,0:T(1,128)}) fusion(f32[2,256]{1,0:T(2,128)S(1)} %shard_map.122), kind=kLoop, calls=%fused_computation | loop fusion | bytes 4096 | tf_op jit(solution)/shard_map/slice | solution.py:861
